TPU v7x, 512 devices: a whole 4x4x16 slice. The times are simulated.
512 devices in a mesh: hist: 256 (over z, x, y_lo, core), orb: 2 (over y_hi).
Axes of the slice: x: 4, y: 4 (y_hi: 2, y_lo: 2; y = y_hi * 2 + y_lo), z: 16, core: 2. Of those that a mesh axis runs over, the one named last changes fastest.
Arguments:
- g_hist: bfloat16 [512, 64, 32768], P('hist', 'orb'), may hold values from -6 to 6
- sigma_hist: bfloat16 [2, 64, 32768], P(None, None, 'hist'), may hold values from -0.03125 to 0.03125
- diag_inv: float32 [512, 64, 64], P('hist'), may hold values from -0.75 to 0.75
- previous: float32 [2, 512, 64, 64], P(None, 'hist', 'orb'), may hold values from -6 to 6
- block_of_slot: int32 [256], replicated, may hold values from 0 to 255, each once
- front_pos: int32 [2], replicated, may hold values from 256 to 511
Outputs:
- g_row: float32 [2, 512, 64, 64], P(None, 'hist', 'orb')
- sigma_row: float32 [2, 512, 64, 64], P(None, 'hist', 'orb')
Inputs may be any that keep to these rules, and one draw needn't show every extreme that they name: `block_of_slot`: every block index appears once.
All inputs are finite; a program needn't handle non-finite values.
Results may differ from a plain program's by a relative error of at most 0.0003.
Values may be sent and summed in bfloat16 or wider, within the bound.
No kernel may reach another device: no remote copies, remote signals or barrier semaphores. Data moves between devices by JAX's collectives and lax.ppermute only.
A program may use at most 64 MiB of HBM per device.

v0:
```python
import jax
import jax.numpy as jnp
from jax import lax
from jax.sharding import Mesh
from jax.sharding import PartitionSpec as P

HIST = ("hist_0", "hist_1", "hist_2", "hist_3")


COUPLING = 0.5


def from_root(value, axes, root):
    value = jnp.where(lax.axis_index(axes) == root, value, jnp.zeros_like(value))
    for axis in axes:
        value = lax.psum(value, axis)
    return value


def from_everyone(value, axis):
    count = lax.axis_size(axis)
    return lax.all_to_all(
        jnp.broadcast_to(value[None], (count, *value.shape)), axis, 0, 0, tiled=True
    )


def joined_along(blocks, dim):
    blocks = jnp.moveaxis(blocks, 0, dim)
    lengths = blocks.shape
    return blocks.reshape(*lengths[:dim], lengths[dim] * lengths[dim + 1], *lengths[dim + 2 :])


def gathered_copies(value, axis, dim):
    blocks = from_everyone(value, axis)
    return joined_along(blocks, dim)


def contract(g_piece, s_piece, times, col_time, front_pos):
    g_kept = jnp.where(
        (times[None, :] >= col_time[:, None])[:, None, :], g_piece, jnp.zeros_like(g_piece)
    )
    s_kept = jnp.where(
        (times[None, :] <= front_pos[:, None])[:, None, :], s_piece, jnp.zeros_like(s_piece)
    )
    return jnp.einsum("tcx,fax->ftca", g_kept, s_kept, preferred_element_type=jnp.float32)


def inverse_row(diag_inv, when, col_count):
    local = lax.dynamic_index_in_dim(diag_inv, when % col_count, 0, keepdims=False)
    return from_root(local, HIST, when // col_count)


def body(g_hist, sigma_hist, diag_inv, previous, block_of_slot, front_pos):
    col_count = g_hist.shape[0]
    half_cols = g_hist.shape[1]
    orb_width = sigma_hist.shape[1]
    orb_id = lax.axis_index("orb")
    slot_id = lax.axis_index(HIST)
    my_block = lax.dynamic_index_in_dim(block_of_slot, slot_id, 0, keepdims=False)
    col_time = my_block * col_count + jnp.arange(col_count, dtype=jnp.int32)
    piece = lax.all_gather(sigma_hist, HIST, axis=2, tiled=True)
    count = piece.shape[2]
    times = jnp.arange(count, dtype=jnp.int32) // orb_width
    integral = contract(g_hist, piece, times, col_time, front_pos)
    combined = previous + integral
    rows = jnp.stack([inverse_row(diag_inv, front_pos[front], col_count) for front in range(2)])
    g_row = jnp.einsum("ftcb,fab->ftca", combined, rows, precision=lax.Precision.HIGHEST)
    whole = gathered_copies(g_row, "orb", 2)
    mirror = jnp.swapaxes(lax.dynamic_slice_in_dim(whole, orb_id * half_cols, half_cols, 3), 2, 3)
    sigma_row = COUPLING * g_row * g_row * mirror
    return (g_row, sigma_row)


def solution(mesh):
    split = Mesh(
        mesh.devices.reshape(16, 4, 2, 2, mesh.shape["orb"]),
        ("hist_0", "hist_1", "hist_2", "hist_3", "orb"),
    )
    in_specs = (
        P(HIST, "orb", None),
        P(None, None, HIST),
        P(HIST, None, None),
        P(None, HIST, "orb", None),
        P(),
        P(),
    )
    out_specs = (P(None, HIST, "orb", None), P(None, HIST, "orb", None))
    return jax.shard_map(body, mesh=split, in_specs=in_specs, out_specs=out_specs, check_vma=False)
```

profile of v0, /device:TPU:2, one launch (start us, length us, event | category | flops | bytes accessed | tf_op | source)
XLA Modules:
  0.0 462.0 jit_solution(15964508195874430775)
XLA Ops:
  7.2 0.0 all-gather.2.cloned.1.call-start
  7.2 0.7 all-gather.2.cloned.1.call-update
  7.9 1.3 fusion.28
  14.5 1.3 dynamic_slice.14
  16.4 0.8 select_bitcast_fusion.1
  17.2 62.1 %all-reduce = (f32[64,64]{1,0:T(8,128)S(1)}, f32[64,64]{1,0:T(8,128)S(1)}) all-reduce(f32[64,64]{1,0:T(8,128)S(1)} %get-tuple-element.13, f32[64,64]{1,0:T(8,128)S(1)} %get-tuple-element.12), channel_id=1, replica_groups=mesh['hist_0'=16,'hist_1'=4,'hist_2'=2,'hist_3'=2,'orb'=2] {'hist_0'}, use_global_device_ids=true, to_apply=%region_4.5 | all-reduce | flops 8192 | bytes 65536 | tf_op jit(solution)/shard_map/psum | solution.py:16
  79.3 14.6 %all-reduce.1 = (f32[64,64]{1,0:T(8,128)S(1)}, f32[64,64]{1,0:T(8,128)S(1)}) all-reduce(f32[64,64]{1,0:T(8,128)S(1)} %get-tuple-element.2, f32[64,64]{1,0:T(8,128)S(1)} %get-tuple-element.3), channel_id=1, replica_groups=mesh['hist_0'=16,'hist_1'=4,'hist_2'=2,'hist_3'=2,'orb'=2] {'hist_1'}, use_global_device_ids=true, to_apply=%region_5.6 | all-reduce | flops 8192 | bytes 65536 | tf_op jit(solution)/shard_map/psum | solution.py:16
  94.0 8.9 %all-reduce.3 = (f32[64,64]{1,0:T(8,128)S(1)}, f32[64,64]{1,0:T(8,128)S(1)}) all-reduce(f32[64,64]{1,0:T(8,128)S(1)} %get-tuple-element.4, f32[64,64]{1,0:T(8,128)S(1)} %get-tuple-element.5), channel_id=1, replica_groups=mesh['hist_0'=16,'hist_1'=4,'hist_2'=2,'hist_3'=2,'orb'=2] {'hist_2'}, use_global_device_ids=true, to_apply=%region_6.7 | all-reduce | flops 8192 | bytes 65536 | tf_op jit(solution)/shard_map/psum | solution.py:16
  102.9 3.6 all-reduce.2
  106.6 1.0 broadcast_compare_fusion.1
  107.6 325.5 %all-gather.2.cloned.1.call-done = bf16[2,64,32768]{2,1,0:T(8,128)(2,1)} async-done(((bf16[2,64,128]{2,1,0:T(8,128)(2,1)}), bf16[2,64,32768]{2,1,0:T(8,128)(2,1)}) %all-gather.2.cloned.1.call-update) | async-done | bytes 8388624 | tf_op jit(solution)/shard_map/all_gather | solution.py:61
  433.0 8.8 %fusion.14 = f32[2,2,32,64]{3,2,1,0:T(8,128)S(1)} fusion(f32[2,2,32,64]{3,2,1,0:T(8,128)} %param.9, bf16[2,32,32768]{2,1,0:T(8,128)(2,1)} %param.6, pred[2,32768]{1,0:T(4,128)(4,1)S(1)} %get-tuple-element.11, bf16[2,64,32768]{2,1,0:T(8,128)(2,1)} %all-gather.2.cloned.1.call-done, pred[2,32768]{1,0:T(4,128)(4,1)S(1)} %get-tuple-element.10), kind=kOutput, calls=%fused_computation.10 | convolution fusion | flops 543170560 | bytes 12779520 | tf_op jit(solution)/shard_map/tcx,fax->ftca/dot_general | solution.py:45
  441.8 0.2 fusion.23
  442.0 0.0 copy-start
  442.1 0.8 reshape.83
  442.8 4.3 all-to-all-start
  447.2 5.6 %all-to-all-done = f32[2,1,8192]{2,1,0:T(1,128)S(1)} async-done(((f32[2,1,8192]{2,1,0:T(1,128)}), f32[2,1,8192]{2,1,0:T(1,128)S(1)}, u32[]{:S(2)}, u32[]{:S(2)}) %all-to-all-start) | async-done | bytes 65568 | tf_op jit(solution)/shard_map/all_to_all | solution.py:22
  452.8 0.5 broadcast.82
  453.3 0.8 reduce
  454.1 0.1 reshape.84
  454.3 0.1 constant_dynamic-slice_fusion
  454.4 0.1 copy.14
  454.5 0.6 fusion.22
  455.1 0.0 copy-done
  (4 shorter events, 0.0 us)
Async XLA Ops:
  7.2 425.9 %all-gather.2.cloned.1.call-start = ((), (), s32[]{:S(2)}) async-start(), calls=%async_computation.1 | async-start | bytes 8421376 | tf_op jit(solution)/shard_map/all_gather | solution.py:61
  442.0 13.1 %copy-start = (f32[2,2,32,64]{3,2,1,0:T(8,128)}, f32[2,2,32,64]{3,2,1,0:T(8,128)S(1)}, u32[]{:S(2)}) copy-start(f32[2,2,32,64]{3,2,1,0:T(8,128)S(1)} %fusion.23) | copy-start | bytes 98308
  442.8 9.9 %all-to-all-start = ((f32[2,1,8192]{2,1,0:T(1,128)}), f32[2,1,8192]{2,1,0:T(1,128)S(1)}, u32[]{:S(2)}, u32[]{:S(2)}) async-start(f32[2,1,8192]{2,1,0:T(1,128)} %reshape.83), calls=%async_computation | async-start | bytes 131072 | tf_op jit(solution)/shard_map/all_to_all | solution.py:22
Sparse Core Ops, SparseCore 0:
  10.1 422.8 all-gather.1
where the time goes:
time: 462 us
  waiting for transfers between devices  332 us (72%)
  blocking collectives  89.3 us (19%)
  between operations  20 us (4%)
  matrix products  9 us (2%)
    all_gather x1, waiting for transfers between devices, body(): piece = lax.all_gather(sigma_hist, HIST, axis=2, tiled=True)  325 us
    psum x4, blocking collectives, from_root(): value = lax.psum(value, axis)  89.3 us
  transfers between devices with their start and end apart: 2, of which 2 were waited for; matrix products, arithmetic and copies ran while one was open for 1% of the time, Pallas kernels for 0%

commit v1 on v0

v1 whole, which is shorter than its diff:
```python
import jax
import jax.numpy as jnp
from jax import lax
from jax.experimental import pallas as pl
from jax.experimental.pallas import tpu as pltpu
from jax.sharding import Mesh
from jax.sharding import PartitionSpec as P

HIST = ("z", "x", "yl", "core")
RING = ("yl", "yh")
COUPLING = 0.5
SPLIT_ROWS = 32
F32 = jnp.float32
BF16 = jnp.bfloat16
VMEM = pltpu.VMEM
SMEM = pltpu.SMEM


def whole(space=VMEM):
    return pl.BlockSpec(memory_space=space)


def ring_index(y):
    return (y % 2) * 2 + y // 2


def prep_kernel(slots, fronts, g_ref, sigma_ref, inv_ref, *outs):
    piece_refs, share_ref, chunk_ref = outs[:4], outs[4], outs[5]
    pair = pl.program_id(0)
    yl, core, yh = lax.axis_index("yl"), lax.axis_index("core"), lax.axis_index("yh")
    hist = ((lax.axis_index("z") * 4 + lax.axis_index("x")) * 2 + yl) * 2 + core
    first = slots[hist] * 2
    lane = lax.broadcasted_iota(jnp.int32, (64, 128), 1)
    row = lax.broadcasted_iota(jnp.int32, (64, 128), 0)
    upper = (lane >= 64).astype(jnp.int32)
    ahead = pair * 64 + upper * 32 - first - (row >= 32).astype(jnp.int32)
    pick_in = lax.broadcasted_iota(jnp.int32, (256, 128), 0)
    pick_out = lax.broadcasted_iota(jnp.int32, (256, 128), 1)
    pick_out = pick_out + 64 * (pick_out >= 64).astype(jnp.int32)
    for d in range(4):
        y = (yh * 2 + yl + d) % 4
        to_yl, to_yh = y % 2, y // 2
        pick = jnp.where(pick_in == pick_out + 64 * to_yh, 1.0, 0.0).astype(BF16)
        blocks = []
        for h in range(2):
            to_core = core if h == 0 else 1 - core
            for x in range(4):
                at = (x * 4 + to_yl * 2 + to_core) * 128
                even = g_ref[:, pl.ds(pl.multiple_of(at, 128), 128)]
                odd = g_ref[:, pl.ds(pl.multiple_of(at + 2048, 128), 128)]
                blocks.append(jnp.concatenate([even, odd], axis=1))
        picked = jnp.dot(jnp.concatenate(blocks, axis=0), pick, preferred_element_type=F32)
        for h in range(2):
            to_core = core if h == 0 else 1 - core
            for x in range(4):
                at = h * 4 + x
                term = x * 8 + to_yl * 4 + to_core * 2 + to_yh
                kept = jnp.where(ahead + term >= 0, picked[at * 64 : at * 64 + 64], 0.0)
                piece_refs[d][at] = kept.astype(BF16)

    @pl.when(pair == 0)
    def _():
        flipped = sigma_ref[...].astype(F32).T
        mine = jnp.where(yh == 0, flipped[:64], flipped[64:])
        limit = jnp.where(upper > 0, fronts[1], fronts[0])
        chunk_ref[...] = jnp.where(2 * hist + yh <= limit, mine, 0.0).astype(BF16)
        when = jnp.where(yh == 0, fronts[0], fronts[1])
        block = jnp.where(when % 2 == 0, inv_ref[0], inv_ref[1])
        block = jnp.where(when // 2 == hist, block, 0.0)
        share_ref[:, :64] = block[:32]
        share_ref[:, 64:] = block[32:]


def prep(slots, fronts, g_hist, sigma_hist, diag_inv):
    return pl.pallas_call(
        prep_kernel,
        grid=(8,),
        in_specs=[
            whole(SMEM),
            whole(SMEM),
            pl.BlockSpec((64, 4096), lambda i: (0, i)),
            pl.BlockSpec((128, 128), lambda i: (0, 0)),
            pl.BlockSpec((2, 64, 64), lambda i: (0, 0, 0)),
        ],
        out_specs=[pl.BlockSpec((8, 64, 128), lambda i: (0, 0, i))] * 4
        + [pl.BlockSpec((32, 128), lambda i: (0, 0)), pl.BlockSpec((64, 128), lambda i: (0, 0))],
        out_shape=[jax.ShapeDtypeStruct((8, 64, 1024), BF16)] * 4
        + [jax.ShapeDtypeStruct((32, 128), F32), jax.ShapeDtypeStruct((64, 128), BF16)],
        name="prep",
    )(slots, fronts, g_hist, sigma_hist, diag_inv)


def along_z_kernel(shares_ref, chunk_ref, out_ref):
    core = lax.axis_index("core")
    share = shares_ref[0] + shares_ref[1]
    mine = jnp.where(core == 0, share[:16], share[16:])
    high = mine.astype(BF16)
    low = (mine - high.astype(F32)).astype(BF16)
    message = jnp.concatenate([chunk_ref[...], high, low], axis=0)
    for z in range(16):
        out_ref[z] = message


def along_x_kernel(in_ref, out_ref):
    share = in_ref[0, 64:].astype(F32)
    for z in range(1, 16):
        share = share + in_ref[z, 64:].astype(F32)
    share = share.astype(BF16)
    for x in range(4):
        for z in range(16):
            out_ref[x, z * 64 : z * 64 + 64] = in_ref[z, :64]
        out_ref[x, 1024:] = share


def first_kernel(s_ref, g0, g1, g2, g3, out_ref):
    rows = jnp.concatenate([g0[0], g1[0], g2[0], g3[0]], axis=0)
    part = jnp.dot(rows, s_ref[0, :1024], preferred_element_type=F32)

    @pl.when(pl.program_id(0) == 0)
    def _():
        out_ref[...] = part

    @pl.when(pl.program_id(0) > 0)
    def _():
        out_ref[...] += part


def second_kernel(s_ref, g0, g1, g2, g3, part_ref, mine_ref, other_ref, prev_ref, out_ref, total):
    rows = jnp.concatenate([g0[0], g1[0], g2[0], g3[0]], axis=0)
    part = jnp.dot(rows, s_ref[0, :1024], preferred_element_type=F32).reshape(4, 64, 128)
    step = pl.program_id(0)

    @pl.when(step == 0)
    def _():
        total[...] = part + part_ref[...]

    @pl.when(step > 0)
    def _():
        total[...] += part

    @pl.when(step == 3)
    def _():
        core, yl, yh = lax.axis_index("core"), lax.axis_index("yl"), lax.axis_index("yh")
        before = [prev_ref[f].reshape(64, 64) for f in range(2)]
        total[0] += jnp.concatenate(before, axis=1)

        def joined(ref):
            halves = ref[...].astype(F32)
            halves = halves[0] + halves[1] + halves[2] + halves[3]
            return halves[:16] + halves[16:]

        mine, other = joined(mine_ref), joined(other_ref)
        share = jnp.concatenate(
            [jnp.where(core == 0, mine, other), jnp.where(core == 0, other, mine)], axis=0
        )
        for to in range(4):
            for half in range(2):
                d = (yh * 2 + yl + 4 - (half * 2 + to // 2)) % 4
                out_ref[to, half * 64 : half * 64 + 64] = total[d]
            out_ref[to, 128:] = share


def dots(s, pieces, half, extra=(), extra_specs=(), kernel=first_kernel, out=(256, 128), scratch=()):
    return pl.pallas_call(
        kernel,
        grid=(4,),
        in_specs=[pl.BlockSpec((1, 1056, 128), lambda i: (i, 0, 0))]
        + [pl.BlockSpec((1, 64, 1024), lambda i: (half * 4 + i, 0, 0))] * 4
        + list(extra_specs),
        out_specs=pl.BlockSpec(out, lambda i: (0,) * len(out)),
        out_shape=jax.ShapeDtypeStruct(out, F32),
        scratch_shapes=list(scratch),
        cost_estimate=pl.CostEstimate(
            flops=2 * 256 * 4096 * 128, bytes_accessed=3 << 20, transcendentals=0
        ),
        name=kernel.__name__,
    )(s, *pieces, *extra)


def last_kernel(in_ref, g_ref, s_ref):
    yh = lax.axis_index("yh")
    combined = in_ref[0, :128] + in_ref[1, :128] + in_ref[2, :128] + in_ref[3, :128]
    for f in range(2):
        share = in_ref[f, 128:] + in_ref[2 + f, 128:]
        rows = jnp.concatenate([share[:, :64], share[:, 64:]], axis=0)
        g = lax.dot_general(
            combined[:, f * 64 : f * 64 + 64],
            rows,
            (((1,), (1,)), ((), ())),
            precision=lax.Precision.HIGHEST,
            preferred_element_type=F32,
        )
        for r in range(2):
            low, high = g[r * 32 : r * 32 + 32], g[64 + r * 32 : 96 + r * 32]
            flipped = jnp.concatenate([low, high], axis=0).T
            mirror = jnp.where(yh == 0, flipped[:32], flipped[32:])
            mine = jnp.where(yh == 0, low, high)
            g_ref[f, r] = mine
            s_ref[f, r] = COUPLING * mine * mine * mirror


def body(g_hist, sigma_hist, diag_inv, previous, block_of_slot, front_pos):
    *pieces, share, chunk = prep(
        block_of_slot,
        front_pos,
        g_hist.reshape(64, 32768),
        sigma_hist.reshape(128, 128),
        diag_inv,
    )
    rows = [pieces[0]]
    for d in (2, 1, 3):
        pairs = [(ring_index(y), ring_index((y + d) % 4)) for y in range(4)]
        rows.append(lax.ppermute(pieces[d], RING, pairs))
    rows = [rows[0], rows[2], rows[1], rows[3]]
    shares = lax.all_gather(share, "core")
    message = pl.pallas_call(
        along_z_kernel,
        in_specs=[whole(), whole()],
        out_specs=whole(),
        out_shape=jax.ShapeDtypeStruct((16, 96, 128), BF16),
        name="along_z",
    )(shares, chunk)
    message = lax.all_to_all(message, "z", 0, 0, tiled=True)
    message = pl.pallas_call(
        along_x_kernel,
        in_specs=[whole()],
        out_specs=whole(),
        out_shape=jax.ShapeDtypeStruct((4, 1056, 128), BF16),
        name="along_x",
    )(message)
    mine = lax.all_to_all(message, "x", 0, 0, tiled=True)
    other = lax.ppermute(mine, "core", [(0, 1), (1, 0)])
    part = dots(mine, rows, 0)
    tail = pl.BlockSpec((4, SPLIT_ROWS, 128), lambda i: (0, 1024 // SPLIT_ROWS, 0))
    sums = dots(
        other,
        rows,
        1,
        (part.reshape(4, 64, 128), mine, other, previous),
        (
            pl.BlockSpec((4, 64, 128), lambda i: (0, 0, 0)),
            tail,
            tail,
            pl.BlockSpec((2, 2, 32, 64), lambda i: (0, 0, 0, 0)),
        ),
        second_kernel,
        (4, 160, 128),
        (VMEM((4, 64, 128), F32),),
    )
    sums = lax.all_to_all(sums, RING, 0, 0, tiled=True)
    out = jax.ShapeDtypeStruct(previous.shape, F32)
    return pl.pallas_call(
        last_kernel,
        in_specs=[whole()],
        out_specs=(whole(), whole()),
        out_shape=(out, out),
        name="last",
    )(sums)


def solution(mesh):
    split = Mesh(mesh.devices.reshape(16, 4, 2, 2, 2), (*HIST, "yh"))
    in_specs = (
        P(HIST, "yh", None),
        P(None, None, HIST),
        P(HIST, None, None),
        P(None, HIST, "yh", None),
        P(),
        P(),
    )
    out_specs = (P(None, HIST, "yh", None), P(None, HIST, "yh", None))
    return jax.shard_map(body, mesh=split, in_specs=in_specs, out_specs=out_specs, check_vma=False)
```

time: 462 us -> 152 us (0.33)
  the two profiles are of different devices: /device:TPU:2 before, /device:TPU:32 now
where the time goes in v1:
time: 152 us; the launch traced here: 151 us
  blocking collectives  71.7 us (47%)
  waiting for transfers between devices  42.3 us (28%)
  Pallas kernels  22.2 us (15%)
  starting transfers between devices  13.5 us (9%)
    ppermute x3, waiting for transfers between devices, body(): rows.append(lax.ppermute(pieces[d], RING, pairs))  42.3 us
    all_to_all x1, blocking collectives, body(): message = lax.all_to_all(message, 'z', 0, 0, tiled=True)  37.6 us
    all_to_all x1, blocking collectives, body(): mine = lax.all_to_all(message, 'x', 0, 0, tiled=True)  19.6 us
    ppermute x3, starting transfers between devices, body(): rows.append(lax.ppermute(pieces[d], RING, pairs))  11.6 us
    all_to_all x1, blocking collectives, body(): sums = lax.all_to_all(sums, RING, 0, 0, tiled=True)  11.4 us
    pallas_call x1, Pallas kernels, prep(): pl.pallas_call(prep_kernel, grid=(8,), in_specs=[whole(SMEM), whole(SMEM)...  8.42 us
    pallas_call x2, Pallas kernels, dots(): pl.pallas_call(kernel, grid=(4,), in_specs=[pl.BlockSpec((1, 1056, 128),...  8.11 us
    all_gather x1, blocking collectives, body(): shares = lax.all_gather(share, 'core')  3.15 us
  transfers between devices with their start and end apart: 4, of which 3 were waited for; matrix products, arithmetic and copies ran while one was open for 0% of the time, Pallas kernels for 3%

profile of v1, /device:TPU:32, one launch (start us, length us, event | category | flops | bytes accessed | tf_op | source)
XLA Modules:
  0.0 151.3 jit_solution(9948991490620594940)
XLA Ops:
  0.6 8.4 %prep.1 = (bf16[8,64,1024]{2,1,0:T(8,128)(2,1)}, bf16[8,64,1024]{2,1,0:T(8,128)(2,1)}, bf16[8,64,1024]{2,1,0:T(8,128)(2,1)}, bf16[8,64,1024]{2,1,0:T(8,128)(2,1)...) custom-call(s32[256]{0:T(256)} %slots.1, s32[2]{0:T(128)} %fronts.1, bf16[64,32768]{1,0:T(8,128)(2,1)} %bitcast.4, ...), custom_call_target="tpu_custom_call" | custom-call | tf_op jit(solution)/shard_map/prep/pallas_call | solution.py:75
  9.0 3.2 %all-gather = f32[64,128]{1,0:T(8,128)} all-gather(f32[32,128]{1,0:T(8,128)} %get-tuple-element.8), channel_id=2, replica_groups=mesh['z'=16,'x'=4,'yl'=2,'core'=2,'yh'=2] {'core'}, dimensions={0}, use_global_device_ids=true | all-gather | bytes 49152 | tf_op jit(solution)/shard_map/all_gather | solution.py:215
  12.2 1.5 %along_z.1 = bf16[16,96,128]{2,1,0:T(8,128)(2,1)} custom-call(f32[2,32,128]{2,1,0:T(8,128)} %bitcast.6, bf16[64,128]{1,0:T(8,128)(2,1)} %get-tuple-element.9.chunk_ref), custom_call_target="tpu_custom_call" | custom-call | tf_op jit(solution)/shard_map/along_z/pallas_call | solution.py:216
  13.7 37.6 %all_to_all.15.in_ref = bf16[16,96,128]{2,1,0:T(8,128)(2,1)} all-to-all(bf16[16,96,128]{2,1,0:T(8,128)(2,1)} %along_z.1), channel_id=1, replica_groups=mesh['z'=16,'x'=4,'yl'=2,'core'=2,'yh'=2] {'z'}, dimensions={0} | all-to-all | bytes 786432 | tf_op jit(solution)/shard_map/all_to_all | solution.py:223
  51.3 2.1 %along_x.1 = bf16[4,1056,128]{2,1,0:T(8,128)(2,1)} custom-call(bf16[16,96,128]{2,1,0:T(8,128)(2,1)} %all_to_all.15.in_ref), custom_call_target="tpu_custom_call" | custom-call | tf_op jit(solution)/shard_map/along_x/pallas_call | solution.py:224
  53.5 0.0 copy-start.4
  53.5 0.0 copy-start.3
  53.5 19.6 %all_to_all.16.s_ref.mine_ref = bf16[4,1056,128]{2,1,0:T(8,128)(2,1)S(1)} all-to-all(bf16[4,1056,128]{2,1,0:T(8,128)(2,1)} %along_x.1), channel_id=1, replica_groups=mesh['z'=16,'x'=4,'yl'=2,'core'=2,'yh'=2] {'x'}, dimensions={0} | all-to-all | bytes 2162688 | tf_op jit(solution)/shard_map/all_to_all | solution.py:231
  73.0 0.0 copy-start
  73.0 1.9 %collective-permute-start = (bf16[4,1056,128]{2,1,0:T(8,128)(2,1)S(1)}, bf16[4,1056,128]{2,1,0:T(8,128)(2,1)S(1)}, u32[]{:S(2)}, u32[]{:S(2)}) collective-permute-start(bf16[4,1056,128]{2,1,0:T(8,128)(2,1)S(1)} %all_to_all.16.s_ref.mine_ref), channel_id=1, source_target_pairs={{0,2},{2,0},{1,3},{3,1},{4,6},{6,4},{5,7},{7,5},{8,10},{10,8},{9,1... | collective-permute-start | bytes 3244040 | tf_op jit(solution)/shard_map/ppermute | solution.py:232
  74.9 3.5 %collective-permute-start.1 = (bf16[8,64,1024]{2,1,0:T(8,128)(2,1)}, bf16[8,64,1024]{2,1,0:T(8,128)(2,1)S(1)}, u32[]{:S(2)}, u32[]{:S(2)}) collective-permute-start(bf16[8,64,1024]{2,1,0:T(8,128)(2,1)} %get-tuple-element.11), channel_id=1, source_target_pairs={{0,4},{4,1},{1,5},{5,0},{2,6},{6,3},{3,7},{7,2},{8,12},{12,9},{9,1... | collective-permute-start | bytes 3145736 | tf_op jit(solution)/shard_map/ppermute | solution.py:213
  78.4 0.0 copy-done.4
  78.5 4.8 %collective-permute-start.2 = (bf16[8,64,1024]{2,1,0:T(8,128)(2,1)S(1)}, bf16[8,64,1024]{2,1,0:T(8,128)(2,1)}, u32[]{:S(2)}, u32[]{:S(2)}) collective-permute-start(bf16[8,64,1024]{2,1,0:T(8,128)(2,1)S(1)} %copy-done.4), channel_id=1, source_target_pairs={{0,1},{4,5},{1,0},{5,4},{2,3},{6,7},{3,2},{7,6},{8,9},{12,13},{9,8... | collective-permute-start | bytes 3145736 | tf_op jit(solution)/shard_map/ppermute | solution.py:213
  83.3 0.0 copy-done.3
  83.3 3.3 %collective-permute-start.3 = (bf16[8,64,1024]{2,1,0:T(8,128)(2,1)S(1)}, bf16[8,64,1024]{2,1,0:T(8,128)(2,1)}, u32[]{:S(2)}, u32[]{:S(2)}) collective-permute-start(bf16[8,64,1024]{2,1,0:T(8,128)(2,1)S(1)} %copy-done.3), channel_id=1, source_target_pairs={{0,5},{4,0},{1,4},{5,1},{2,7},{6,2},{3,6},{7,3},{8,13},{12,8},{9,1... | collective-permute-start | bytes 3145736 | tf_op jit(solution)/shard_map/ppermute | solution.py:213
  86.6 17.4 %collective-permute-done.1.g1 = bf16[8,64,1024]{2,1,0:T(8,128)(2,1)S(1)} collective-permute-done((bf16[8,64,1024]{2,1,0:T(8,128)(2,1)}, bf16[8,64,1024]{2,1,0:T(8,128)(2,1)S(1)}, u32[]{:S(2)}, u32[]{:S(2)}) %collective-permute-start.1) | collective-permute-done | bytes 1048608 | tf_op jit(solution)/shard_map/ppermute | solution.py:213
  103.9 0.0 copy-start.2
  103.9 23.7 %collective-permute-done.2.g2 = bf16[8,64,1024]{2,1,0:T(8,128)(2,1)} collective-permute-done((bf16[8,64,1024]{2,1,0:T(8,128)(2,1)S(1)}, bf16[8,64,1024]{2,1,0:T(8,128)(2,1)}, u32[]{:S(2)}, u32[]{:S(2)}) %collective-permute-start.2) | collective-permute-done | bytes 1048608 | tf_op jit(solution)/shard_map/ppermute | solution.py:213
  127.6 1.2 collective-permute-done.3.g3
  128.8 0.0 copy-done
  128.8 0.0 copy-done.2
  128.8 3.9 %first_kernel.1 = f32[256,128]{1,0:T(8,128)} custom-call(bf16[4,1056,128]{2,1,0:T(8,128)(2,1)} %copy-done, bf16[8,64,1024]{2,1,0:T(8,128)(2,1)} %get-tuple-element.10.g0, bf16[8,64,1024]{2,1,0:T(8,128)(2,1)} %copy-done.2, bf16[8,64,1024]{2,1,0:T(8,128)(2,1)} %collective-permute-done.2.g2, bf16[8,64,1024]{2,1,0:T(8,128)(2,1)} %collective-permute-done.3.g3), custom_call_target="tpu_custom_call" | custom-call | flops 268435456 | bytes 3145728 | tf_op jit(solution)/shard_map/first_kernel/pallas_call | solution.py:164
  132.7 0.0 collective-permute-done.s_ref.other_ref
  132.7 0.0 copy-start.1
  132.7 1.0 copy-done.1
  133.7 4.2 %second_kernel.1 = f32[4,160,128]{2,1,0:T(8,128)} custom-call(bf16[4,1056,128]{2,1,0:T(8,128)(2,1)} %copy-done.1, bf16[8,64,1024]{2,1,0:T(8,128)(2,1)} %get-tuple-element.10.g0, bf16[8,64,1024]{2,1,0:T(8,128)(2,1)} %copy-done.2, bf16[8,64,1024]{2,1,0:T(8,128)(2,1)} %collective-permute-done.2.g2, bf16[8,64,1024]{2,1,0:T(8,128)(2,1)} %collective-permute-done.3.g3, ...), custom_call_target="tpu_custom_call" | custom-call | flops 268435456 | bytes 3145728 | tf_op jit(solution)/shard_map/second_kernel/pallas_call | solution.py:164
  137.9 11.4 %all_to_all.17.in_ref = f32[4,160,128]{2,1,0:T(8,128)} all-to-all(f32[4,160,128]{2,1,0:T(8,128)} %second_kernel.1), channel_id=1, replica_groups=mesh['z'=16,'x'=4,'yl'=2,'core'=2,'yh'=2] {'yl','yh'}, dimensions={0} | all-to-all | bytes 655360 | tf_op jit(solution)/shard_map/all_to_all | solution.py:250
  149.3 2.0 %last.1 = (f32[2,2,32,64]{3,2,1,0:T(8,128)}, f32[2,2,32,64]{3,2,1,0:T(8,128)}) custom-call(f32[4,160,128]{2,1,0:T(8,128)} %all_to_all.17.in_ref), custom_call_target="tpu_custom_call" | custom-call | tf_op jit(solution)/shard_map/last/pallas_call | solution.py:252
Async XLA Ops:
  53.5 25.0 %copy-start.4 = (bf16[8,64,1024]{2,1,0:T(8,128)(2,1)S(1)}, bf16[8,64,1024]{2,1,0:T(8,128)(2,1)}, u32[]{:S(2)}) copy-start(bf16[8,64,1024]{2,1,0:T(8,128)(2,1)} %get-tuple-element.12) | copy-start | bytes 3145732
  53.5 29.8 %copy-start.3 = (bf16[8,64,1024]{2,1,0:T(8,128)(2,1)S(1)}, bf16[8,64,1024]{2,1,0:T(8,128)(2,1)}, u32[]{:S(2)}) copy-start(bf16[8,64,1024]{2,1,0:T(8,128)(2,1)} %get-tuple-element.13) | copy-start | bytes 3145732
  73.0 55.8 %copy-start = (bf16[4,1056,128]{2,1,0:T(8,128)(2,1)}, bf16[4,1056,128]{2,1,0:T(8,128)(2,1)S(1)}, u32[]{:S(2)}) copy-start(bf16[4,1056,128]{2,1,0:T(8,128)(2,1)S(1)} %all_to_all.16.s_ref.mine_ref) | copy-start | bytes 3244036
  73.0 59.7 %collective-permute-start = (bf16[4,1056,128]{2,1,0:T(8,128)(2,1)S(1)}, bf16[4,1056,128]{2,1,0:T(8,128)(2,1)S(1)}, u32[]{:S(2)}, u32[]{:S(2)}) collective-permute-start(bf16[4,1056,128]{2,1,0:T(8,128)(2,1)S(1)} %all_to_all.16.s_ref.mine_ref), channel_id=1, source_target_pairs={{0,2},{2,0},{1,3},{3,1},{4,6},{6,4},{5,7},{7,5},{8,10},{10,8},{9,1... | collective-permute-start | bytes 3244040 | tf_op jit(solution)/shard_map/ppermute | solution.py:232
  74.9 29.0 %collective-permute-start.1 = (bf16[8,64,1024]{2,1,0:T(8,128)(2,1)}, bf16[8,64,1024]{2,1,0:T(8,128)(2,1)S(1)}, u32[]{:S(2)}, u32[]{:S(2)}) collective-permute-start(bf16[8,64,1024]{2,1,0:T(8,128)(2,1)} %get-tuple-element.11), channel_id=1, source_target_pairs={{0,4},{4,1},{1,5},{5,0},{2,6},{6,3},{3,7},{7,2},{8,12},{12,9},{9,1... | collective-permute-start | bytes 3145736 | tf_op jit(solution)/shard_map/ppermute | solution.py:213
  78.5 49.2 %collective-permute-start.2 = (bf16[8,64,1024]{2,1,0:T(8,128)(2,1)S(1)}, bf16[8,64,1024]{2,1,0:T(8,128)(2,1)}, u32[]{:S(2)}, u32[]{:S(2)}) collective-permute-start(bf16[8,64,1024]{2,1,0:T(8,128)(2,1)S(1)} %copy-done.4), channel_id=1, source_target_pairs={{0,1},{4,5},{1,0},{5,4},{2,3},{6,7},{3,2},{7,6},{8,9},{12,13},{9,8... | collective-permute-start | bytes 3145736 | tf_op jit(solution)/shard_map/ppermute | solution.py:213
  83.3 45.5 %collective-permute-start.3 = (bf16[8,64,1024]{2,1,0:T(8,128)(2,1)S(1)}, bf16[8,64,1024]{2,1,0:T(8,128)(2,1)}, u32[]{:S(2)}, u32[]{:S(2)}) collective-permute-start(bf16[8,64,1024]{2,1,0:T(8,128)(2,1)S(1)} %copy-done.3), channel_id=1, source_target_pairs={{0,5},{4,0},{1,4},{5,1},{2,7},{6,2},{3,6},{7,3},{8,13},{12,8},{9,1... | collective-permute-start | bytes 3145736 | tf_op jit(solution)/shard_map/ppermute | solution.py:213
  103.9 24.9 %copy-start.2 = (bf16[8,64,1024]{2,1,0:T(8,128)(2,1)}, bf16[8,64,1024]{2,1,0:T(8,128)(2,1)S(1)}, u32[]{:S(2)}) copy-start(bf16[8,64,1024]{2,1,0:T(8,128)(2,1)S(1)} %collective-permute-done.1.g1) | copy-start | bytes 3145732
  132.7 1.0 copy-start.1

commit v2 on v1

--- a/solution.py
+++ b/solution.py
@@ -9,6 +9,7 @@
 HIST = ("z", "x", "yl", "core")
 RING = ("yl", "yh")
 COUPLING = 0.5
+PAIRS = 2
 SPLIT_ROWS = 32
 F32 = jnp.float32
 BF16 = jnp.bfloat16
@@ -26,39 +27,45 @@
 
 def prep_kernel(slots, fronts, g_ref, sigma_ref, inv_ref, *outs):
     piece_refs, share_ref, chunk_ref = outs[:4], outs[4], outs[5]
-    pair = pl.program_id(0)
+    step = pl.program_id(0)
     yl, core, yh = lax.axis_index("yl"), lax.axis_index("core"), lax.axis_index("yh")
     hist = ((lax.axis_index("z") * 4 + lax.axis_index("x")) * 2 + yl) * 2 + core
     first = slots[hist] * 2
     lane = lax.broadcasted_iota(jnp.int32, (64, 128), 1)
     row = lax.broadcasted_iota(jnp.int32, (64, 128), 0)
     upper = (lane >= 64).astype(jnp.int32)
-    ahead = pair * 64 + upper * 32 - first - (row >= 32).astype(jnp.int32)
-    pick_in = lax.broadcasted_iota(jnp.int32, (256, 128), 0)
-    pick_out = lax.broadcasted_iota(jnp.int32, (256, 128), 1)
-    pick_out = pick_out + 64 * (pick_out >= 64).astype(jnp.int32)
-    for d in range(4):
+    ahead = upper * 32 - first - (row >= 32).astype(jnp.int32)
+    pick_in = lax.broadcasted_iota(jnp.int32, (256, 256), 0)
+    pick_out = lax.broadcasted_iota(jnp.int32, (256, 256), 1)
+    for d in range(2):
         y = (yh * 2 + yl + d) % 4
         to_yl, to_yh = y % 2, y // 2
-        pick = jnp.where(pick_in == pick_out + 64 * to_yh, 1.0, 0.0).astype(BF16)
-        blocks = []
-        for h in range(2):
-            to_core = core if h == 0 else 1 - core
-            for x in range(4):
-                at = (x * 4 + to_yl * 2 + to_core) * 128
-                even = g_ref[:, pl.ds(pl.multiple_of(at, 128), 128)]
-                odd = g_ref[:, pl.ds(pl.multiple_of(at + 2048, 128), 128)]
-                blocks.append(jnp.concatenate([even, odd], axis=1))
-        picked = jnp.dot(jnp.concatenate(blocks, axis=0), pick, preferred_element_type=F32)
-        for h in range(2):
-            to_core = core if h == 0 else 1 - core
-            for x in range(4):
-                at = h * 4 + x
-                term = x * 8 + to_yl * 4 + to_core * 2 + to_yh
-                kept = jnp.where(ahead + term >= 0, picked[at * 64 : at * 64 + 64], 0.0)
-                piece_refs[d][at] = kept.astype(BF16)
-
-    @pl.when(pair == 0)
+        half = jnp.where(pick_out < 128, to_yh, 1 - to_yh)
+        within = pick_out % 128
+        pick = pick_in == within + 64 * (within >= 64).astype(jnp.int32) + 64 * half
+        pick = jnp.where(pick, 1.0, 0.0).astype(BF16)
+        for p in range(PAIRS):
+            blocks = []
+            for h in range(2):
+                to_core = core if h == 0 else 1 - core
+                for x in range(4):
+                    at = p * 4096 + (x * 4 + to_yl * 2 + to_core) * 128
+                    even = g_ref[:, pl.ds(pl.multiple_of(at, 128), 128)]
+                    odd = g_ref[:, pl.ds(pl.multiple_of(at + 2048, 128), 128)]
+                    blocks.append(jnp.concatenate([even, odd], axis=1))
+            picked = jnp.dot(jnp.concatenate(blocks, axis=0), pick, preferred_element_type=F32)
+            for h in range(2):
+                to_core = core if h == 0 else 1 - core
+                for x in range(4):
+                    at = h * 4 + x
+                    term = (step * PAIRS + p) * 64 + x * 8 + to_yl * 4 + to_core * 2
+                    for far in range(2):
+                        e = 1 - to_yh if far else to_yh
+                        block = picked[at * 64 : at * 64 + 64, far * 128 : far * 128 + 128]
+                        block = jnp.where(ahead + (term + e) >= 0, block, 0.0)
+                        piece_refs[d + 2 * far][at, :, p * 128 : p * 128 + 128] = block.astype(BF16)
+
+    @pl.when(step == 0)
     def _():
         flipped = sigma_ref[...].astype(F32).T
         mine = jnp.where(yh == 0, flipped[:64], flipped[64:])
@@ -74,15 +81,15 @@
 def prep(slots, fronts, g_hist, sigma_hist, diag_inv):
     return pl.pallas_call(
         prep_kernel,
-        grid=(8,),
+        grid=(8 // PAIRS,),
         in_specs=[
             whole(SMEM),
             whole(SMEM),
-            pl.BlockSpec((64, 4096), lambda i: (0, i)),
+            pl.BlockSpec((64, 4096 * PAIRS), lambda i: (0, i)),
             pl.BlockSpec((128, 128), lambda i: (0, 0)),
             pl.BlockSpec((2, 64, 64), lambda i: (0, 0, 0)),
         ],
-        out_specs=[pl.BlockSpec((8, 64, 128), lambda i: (0, 0, i))] * 4
+        out_specs=[pl.BlockSpec((8, 64, 128 * PAIRS), lambda i: (0, 0, i))] * 4
         + [pl.BlockSpec((32, 128), lambda i: (0, 0)), pl.BlockSpec((64, 128), lambda i: (0, 0))],
         out_shape=[jax.ShapeDtypeStruct((8, 64, 1024), BF16)] * 4
         + [jax.ShapeDtypeStruct((32, 128), F32), jax.ShapeDtypeStruct((64, 128), BF16)],
@@ -171,7 +178,7 @@
         out_shape=jax.ShapeDtypeStruct(out, F32),
         scratch_shapes=list(scratch),
         cost_estimate=pl.CostEstimate(
-            flops=2 * 256 * 4096 * 128, bytes_accessed=3 << 20, transcendentals=0
+            flops=(1 << 28) if half else (30 << 30), bytes_accessed=3 << 20, transcendentals=0
         ),
         name=kernel.__name__,
     )(s, *pieces, *extra)

time: 152 us -> 104 us (0.68)
  the two profiles are of different devices: /device:TPU:32 before, /device:TPU:1 now
where the time goes in v2:
time: 104 us; the launch traced here: 103 us
  blocking collectives  35.9 us (35%)
  starting transfers between devices  29.2 us (28%)
  Pallas kernels  19.8 us (19%)
  waiting for transfers between devices  15.6 us (15%)
  local copies, waits for them, and re-layouts  1.72 us (2%)
    all_to_all x1, blocking collectives, body(): mine = lax.all_to_all(message, 'x', 0, 0, tiled=True)  14.3 us
    all_to_all x1, blocking collectives, body(): sums = lax.all_to_all(sums, RING, 0, 0, tiled=True)  11.7 us
    ppermute x3, starting transfers between devices, body(): rows.append(lax.ppermute(pieces[d], RING, pairs))  10.7 us
    all_gather x1, blocking collectives, body(): shares = lax.all_gather(share, 'core')  9.86 us
    all_to_all x1, starting transfers between devices, body(): message = lax.all_to_all(message, 'z', 0, 0, tiled=True)  9.55 us
    ppermute x1, starting transfers between devices, body(): other = lax.ppermute(mine, 'core', [(0, 1), (1, 0)])  8.96 us
    all_to_all x1, waiting for transfers between devices, body(): message = lax.all_to_all(message, 'z', 0, 0, tiled=True)  8.37 us
    pallas_call x2, Pallas kernels, dots(): pl.pallas_call(kernel, grid=(4,), in_specs=[pl.BlockSpec((1, 1056, 128),...  8.12 us
  transfers between devices with their start and end apart: 5, of which 3 were waited for; matrix products, arithmetic and copies ran while one was open for 0% of the time, Pallas kernels for 6%

profile of v2, /device:TPU:1, one launch (start us, length us, event | category | flops | bytes accessed | tf_op | source)
XLA Modules:
  0.0 102.9 jit_solution(7795662674558939459)
XLA Ops:
  0.6 5.9 %prep.1 = (bf16[8,64,1024]{2,1,0:T(8,128)(2,1)}, bf16[8,64,1024]{2,1,0:T(8,128)(2,1)}, bf16[8,64,1024]{2,1,0:T(8,128)(2,1)}, bf16[8,64,1024]{2,1,0:T(8,128)(2,1)...) custom-call(s32[256]{0:T(256)} %slots.1, s32[2]{0:T(128)} %fronts.1, bf16[64,32768]{1,0:T(8,128)(2,1)} %bitcast.4, ...), custom_call_target="tpu_custom_call" | custom-call | tf_op jit(solution)/shard_map/prep/pallas_call | solution.py:82
  6.5 9.9 %all-gather = f32[64,128]{1,0:T(8,128)} all-gather(f32[32,128]{1,0:T(8,128)} %get-tuple-element.8), channel_id=2, replica_groups=mesh['z'=16,'x'=4,'yl'=2,'core'=2,'yh'=2] {'core'}, dimensions={0}, use_global_device_ids=true | all-gather | bytes 49152 | tf_op jit(solution)/shard_map/all_gather | solution.py:222
  16.4 1.6 %along_z.1 = bf16[16,96,128]{2,1,0:T(8,128)(2,1)} custom-call(f32[2,32,128]{2,1,0:T(8,128)} %bitcast.6, bf16[64,128]{1,0:T(8,128)(2,1)} %get-tuple-element.9.chunk_ref), custom_call_target="tpu_custom_call" | custom-call | tf_op jit(solution)/shard_map/along_z/pallas_call | solution.py:223
  18.0 9.6 %all-to-all-start = ((bf16[16,96,128]{2,1,0:T(8,128)(2,1)}), bf16[16,96,128]{2,1,0:T(8,128)(2,1)S(1)}, u32[]{:S(2)}, u32[]{:S(2)}) async-start(bf16[16,96,128]{2,1,0:T(8,128)(2,1)} %along_z.1), calls=%async_computation | async-start | bytes 786432 | tf_op jit(solution)/shard_map/all_to_all | solution.py:230
  27.5 3.2 %collective-permute-start.1 = (bf16[8,64,1024]{2,1,0:T(8,128)(2,1)}, bf16[8,64,1024]{2,1,0:T(8,128)(2,1)S(1)}, u32[]{:S(2)}, u32[]{:S(2)}) collective-permute-start(bf16[8,64,1024]{2,1,0:T(8,128)(2,1)} %get-tuple-element.11), channel_id=1, source_target_pairs={{0,4},{4,1},{1,5},{5,0},{2,6},{6,3},{3,7},{7,2},{8,12},{12,9},{9,1... | collective-permute-start | bytes 3145736 | tf_op jit(solution)/shard_map/ppermute | solution.py:220
  30.7 4.5 %collective-permute-start.2 = (bf16[8,64,1024]{2,1,0:T(8,128)(2,1)}, bf16[8,64,1024]{2,1,0:T(8,128)(2,1)}, u32[]{:S(2)}, u32[]{:S(2)}) collective-permute-start(bf16[8,64,1024]{2,1,0:T(8,128)(2,1)} %get-tuple-element.12), channel_id=1, source_target_pairs={{0,1},{4,5},{1,0},{5,4},{2,3},{6,7},{3,2},{7,6},{8,9},{12,13},{9,8... | collective-permute-start | bytes 3145736 | tf_op jit(solution)/shard_map/ppermute | solution.py:220
  35.3 3.0 %collective-permute-start.3 = (bf16[8,64,1024]{2,1,0:T(8,128)(2,1)}, bf16[8,64,1024]{2,1,0:T(8,128)(2,1)}, u32[]{:S(2)}, u32[]{:S(2)}) collective-permute-start(bf16[8,64,1024]{2,1,0:T(8,128)(2,1)} %get-tuple-element.13), channel_id=1, source_target_pairs={{0,5},{4,0},{1,4},{5,1},{2,7},{6,2},{3,6},{7,3},{8,13},{12,8},{9,1... | collective-permute-start | bytes 3145736 | tf_op jit(solution)/shard_map/ppermute | solution.py:220
  38.3 8.4 %all-to-all-done.in_ref = bf16[16,96,128]{2,1,0:T(8,128)(2,1)S(1)} async-done(((bf16[16,96,128]{2,1,0:T(8,128)(2,1)}), bf16[16,96,128]{2,1,0:T(8,128)(2,1)S(1)}, u32[]{:S(2)}, u32[]{:S(2)}) %all-to-all-start) | async-done | bytes 393248 | tf_op jit(solution)/shard_map/all_to_all | solution.py:230
  46.6 0.0 copy-start.2
  46.6 0.7 copy-done.2
  47.4 2.1 %along_x.1 = bf16[4,1056,128]{2,1,0:T(8,128)(2,1)} custom-call(bf16[16,96,128]{2,1,0:T(8,128)(2,1)} %copy-done.2), custom_call_target="tpu_custom_call" | custom-call | tf_op jit(solution)/shard_map/along_x/pallas_call | solution.py:231
  49.5 14.3 %all_to_all.15.s_ref.mine_ref = bf16[4,1056,128]{2,1,0:T(8,128)(2,1)S(1)} all-to-all(bf16[4,1056,128]{2,1,0:T(8,128)(2,1)} %along_x.1), channel_id=1, replica_groups=mesh['z'=16,'x'=4,'yl'=2,'core'=2,'yh'=2] {'x'}, dimensions={0} | all-to-all | bytes 2162688 | tf_op jit(solution)/shard_map/all_to_all | solution.py:238
  63.8 0.0 copy-start
  63.8 9.0 %collective-permute-start = (bf16[4,1056,128]{2,1,0:T(8,128)(2,1)S(1)}, bf16[4,1056,128]{2,1,0:T(8,128)(2,1)S(1)}, u32[]{:S(2)}, u32[]{:S(2)}) collective-permute-start(bf16[4,1056,128]{2,1,0:T(8,128)(2,1)S(1)} %all_to_all.15.s_ref.mine_ref), channel_id=1, source_target_pairs={{0,2},{2,0},{1,3},{3,1},{4,6},{6,4},{5,7},{7,5},{8,10},{10,8},{9,1... | collective-permute-start | bytes 3244040 | tf_op jit(solution)/shard_map/ppermute | solution.py:239
  72.8 0.0 collective-permute-done.1.g1
  72.8 0.0 copy-start.3
  72.8 6.1 %collective-permute-done.2.g2 = bf16[8,64,1024]{2,1,0:T(8,128)(2,1)} collective-permute-done((bf16[8,64,1024]{2,1,0:T(8,128)(2,1)}, bf16[8,64,1024]{2,1,0:T(8,128)(2,1)}, u32[]{:S(2)}, u32[]{:S(2)}) %collective-permute-start.2) | collective-permute-done | bytes 1048608 | tf_op jit(solution)/shard_map/ppermute | solution.py:220
  78.9 1.1 %collective-permute-done.3.g3 = bf16[8,64,1024]{2,1,0:T(8,128)(2,1)} collective-permute-done((bf16[8,64,1024]{2,1,0:T(8,128)(2,1)}, bf16[8,64,1024]{2,1,0:T(8,128)(2,1)}, u32[]{:S(2)}, u32[]{:S(2)}) %collective-permute-start.3) | collective-permute-done | bytes 1048608 | tf_op jit(solution)/shard_map/ppermute | solution.py:220
  80.1 0.0 copy-done
  80.1 0.0 copy-done.3
  80.1 3.9 %first_kernel.1 = f32[256,128]{1,0:T(8,128)} custom-call(bf16[4,1056,128]{2,1,0:T(8,128)(2,1)} %copy-done, bf16[8,64,1024]{2,1,0:T(8,128)(2,1)} %get-tuple-element.10.g0, bf16[8,64,1024]{2,1,0:T(8,128)(2,1)} %copy-done.3, bf16[8,64,1024]{2,1,0:T(8,128)(2,1)} %collective-permute-done.2.g2, bf16[8,64,1024]{2,1,0:T(8,128)(2,1)} %collective-permute-done.3.g3), custom_call_target="tpu_custom_call" | custom-call | flops 32212254720 | bytes 3145728 | tf_op jit(solution)/shard_map/first_kernel/pallas_call | solution.py:171
  84.0 0.0 collective-permute-done.s_ref.other_ref
  84.0 0.0 copy-start.1
  84.0 1.0 copy-done.1
  85.0 4.2 %second_kernel.1 = f32[4,160,128]{2,1,0:T(8,128)} custom-call(bf16[4,1056,128]{2,1,0:T(8,128)(2,1)} %copy-done.1, bf16[8,64,1024]{2,1,0:T(8,128)(2,1)} %get-tuple-element.10.g0, bf16[8,64,1024]{2,1,0:T(8,128)(2,1)} %copy-done.3, bf16[8,64,1024]{2,1,0:T(8,128)(2,1)} %collective-permute-done.2.g2, bf16[8,64,1024]{2,1,0:T(8,128)(2,1)} %collective-permute-done.3.g3, ...), custom_call_target="tpu_custom_call" | custom-call | flops 268435456 | bytes 3145728 | tf_op jit(solution)/shard_map/second_kernel/pallas_call | solution.py:171
  89.2 11.7 %all_to_all.16.in_ref = f32[4,160,128]{2,1,0:T(8,128)} all-to-all(f32[4,160,128]{2,1,0:T(8,128)} %second_kernel.1), channel_id=1, replica_groups=mesh['z'=16,'x'=4,'yl'=2,'core'=2,'yh'=2] {'yl','yh'}, dimensions={0} | all-to-all | bytes 655360 | tf_op jit(solution)/shard_map/all_to_all | solution.py:257
  100.9 2.0 %last.1 = (f32[2,2,32,64]{3,2,1,0:T(8,128)}, f32[2,2,32,64]{3,2,1,0:T(8,128)}) custom-call(f32[4,160,128]{2,1,0:T(8,128)} %all_to_all.16.in_ref), custom_call_target="tpu_custom_call" | custom-call | tf_op jit(solution)/shard_map/last/pallas_call | solution.py:259
Async XLA Ops:
  18.0 28.7 %all-to-all-start = ((bf16[16,96,128]{2,1,0:T(8,128)(2,1)}), bf16[16,96,128]{2,1,0:T(8,128)(2,1)S(1)}, u32[]{:S(2)}, u32[]{:S(2)}) async-start(bf16[16,96,128]{2,1,0:T(8,128)(2,1)} %along_z.1), calls=%async_computation | async-start | bytes 786432 | tf_op jit(solution)/shard_map/all_to_all | solution.py:230
  27.5 45.2 %collective-permute-start.1 = (bf16[8,64,1024]{2,1,0:T(8,128)(2,1)}, bf16[8,64,1024]{2,1,0:T(8,128)(2,1)S(1)}, u32[]{:S(2)}, u32[]{:S(2)}) collective-permute-start(bf16[8,64,1024]{2,1,0:T(8,128)(2,1)} %get-tuple-element.11), channel_id=1, source_target_pairs={{0,4},{4,1},{1,5},{5,0},{2,6},{6,3},{3,7},{7,2},{8,12},{12,9},{9,1... | collective-permute-start | bytes 3145736 | tf_op jit(solution)/shard_map/ppermute | solution.py:220
  30.7 48.2 %collective-permute-start.2 = (bf16[8,64,1024]{2,1,0:T(8,128)(2,1)}, bf16[8,64,1024]{2,1,0:T(8,128)(2,1)}, u32[]{:S(2)}, u32[]{:S(2)}) collective-permute-start(bf16[8,64,1024]{2,1,0:T(8,128)(2,1)} %get-tuple-element.12), channel_id=1, source_target_pairs={{0,1},{4,5},{1,0},{5,4},{2,3},{6,7},{3,2},{7,6},{8,9},{12,13},{9,8... | collective-permute-start | bytes 3145736 | tf_op jit(solution)/shard_map/ppermute | solution.py:220
  35.3 44.8 %collective-permute-start.3 = (bf16[8,64,1024]{2,1,0:T(8,128)(2,1)}, bf16[8,64,1024]{2,1,0:T(8,128)(2,1)}, u32[]{:S(2)}, u32[]{:S(2)}) collective-permute-start(bf16[8,64,1024]{2,1,0:T(8,128)(2,1)} %get-tuple-element.13), channel_id=1, source_target_pairs={{0,5},{4,0},{1,4},{5,1},{2,7},{6,2},{3,6},{7,3},{8,13},{12,8},{9,1... | collective-permute-start | bytes 3145736 | tf_op jit(solution)/shard_map/ppermute | solution.py:220
  46.6 0.7 copy-start.2
  63.8 16.3 %copy-start = (bf16[4,1056,128]{2,1,0:T(8,128)(2,1)}, bf16[4,1056,128]{2,1,0:T(8,128)(2,1)S(1)}, u32[]{:S(2)}) copy-start(bf16[4,1056,128]{2,1,0:T(8,128)(2,1)S(1)} %all_to_all.15.s_ref.mine_ref) | copy-start | bytes 3244036
  63.8 20.2 %collective-permute-start = (bf16[4,1056,128]{2,1,0:T(8,128)(2,1)S(1)}, bf16[4,1056,128]{2,1,0:T(8,128)(2,1)S(1)}, u32[]{:S(2)}, u32[]{:S(2)}) collective-permute-start(bf16[4,1056,128]{2,1,0:T(8,128)(2,1)S(1)} %all_to_all.15.s_ref.mine_ref), channel_id=1, source_target_pairs={{0,2},{2,0},{1,3},{3,1},{4,6},{6,4},{5,7},{7,5},{8,10},{10,8},{9,1... | collective-permute-start | bytes 3244040 | tf_op jit(solution)/shard_map/ppermute | solution.py:239
  72.8 7.3 %copy-start.3 = (bf16[8,64,1024]{2,1,0:T(8,128)(2,1)}, bf16[8,64,1024]{2,1,0:T(8,128)(2,1)S(1)}, u32[]{:S(2)}) copy-start(bf16[8,64,1024]{2,1,0:T(8,128)(2,1)S(1)} %collective-permute-done.1.g1) | copy-start | bytes 3145732
  84.0 1.0 copy-start.1

commit v3 on v2

--- a/solution.py
+++ b/solution.py
@@ -9,7 +9,7 @@
 HIST = ("z", "x", "yl", "core")
 RING = ("yl", "yh")
 COUPLING = 0.5
-PAIRS = 2
+PAIRS = 4
 SPLIT_ROWS = 32
 F32 = jnp.float32
 BF16 = jnp.bfloat16
@@ -17,8 +17,19 @@
 SMEM = pltpu.SMEM
 
 
+ROOM = pltpu.CompilerParams(vmem_limit_bytes=20 << 20)
+
+
 def whole(space=VMEM):
     return pl.BlockSpec(memory_space=space)
+
+
+def near(value):
+    return pltpu.with_memory_space_constraint(value, VMEM)
+
+
+def far(value):
+    return pltpu.with_memory_space_constraint(value, pltpu.HBM)
 
 
 def ring_index(y):
@@ -91,10 +102,11 @@
         ],
         out_specs=[pl.BlockSpec((8, 64, 128 * PAIRS), lambda i: (0, 0, i))] * 4
         + [pl.BlockSpec((32, 128), lambda i: (0, 0)), pl.BlockSpec((64, 128), lambda i: (0, 0))],
-        out_shape=[jax.ShapeDtypeStruct((8, 64, 1024), BF16)] * 4
-        + [jax.ShapeDtypeStruct((32, 128), F32), jax.ShapeDtypeStruct((64, 128), BF16)],
+        out_shape=[pltpu.HBM((8, 64, 1024), BF16)] * 4
+        + [VMEM((32, 128), F32), VMEM((64, 128), BF16)],
+        compiler_params=ROOM,
         name="prep",
-    )(slots, fronts, g_hist, sigma_hist, diag_inv)
+    )(far(slots), far(fronts), far(g_hist), far(sigma_hist), far(diag_inv))
 
 
 def along_z_kernel(shares_ref, chunk_ref, out_ref):
@@ -175,13 +187,14 @@
         + [pl.BlockSpec((1, 64, 1024), lambda i: (half * 4 + i, 0, 0))] * 4
         + list(extra_specs),
         out_specs=pl.BlockSpec(out, lambda i: (0,) * len(out)),
-        out_shape=jax.ShapeDtypeStruct(out, F32),
+        out_shape=VMEM(out, F32),
         scratch_shapes=list(scratch),
         cost_estimate=pl.CostEstimate(
             flops=(1 << 28) if half else (30 << 30), bytes_accessed=3 << 20, transcendentals=0
         ),
+        compiler_params=ROOM,
         name=kernel.__name__,
-    )(s, *pieces, *extra)
+    )(near(s), *pieces, *[near(value) for value in extra])
 
 
 def last_kernel(in_ref, g_ref, s_ref):
@@ -206,6 +219,33 @@
             s_ref[f, r] = COUPLING * mine * mine * mirror
 
 
+def along_ring(piece, d):
+    return lax.ppermute(piece, RING, [(ring_index(y), ring_index((y + d) % 4)) for y in range(4)])
+
+
+def gathered(share, chunk, first, third):
+    shares = lax.all_gather(share, "core")
+    message = pl.pallas_call(
+        along_z_kernel,
+        in_specs=[whole(), whole()],
+        out_specs=whole(),
+        out_shape=VMEM((16, 96, 128), BF16),
+        compiler_params=ROOM,
+        name="along_z",
+    )(near(shares), near(chunk))
+    message = lax.all_to_all(message, "z", 0, 0, tiled=True)
+    message = pl.pallas_call(
+        along_x_kernel,
+        in_specs=[whole()],
+        out_specs=whole(),
+        out_shape=VMEM((4, 1056, 128), BF16),
+        compiler_params=ROOM,
+        name="along_x",
+    )(near(message))
+    first, third = along_ring(first, 1), along_ring(third, 3)
+    return lax.all_to_all(message, "x", 0, 0, tiled=True), first, third
+
+
 def body(g_hist, sigma_hist, diag_inv, previous, block_of_slot, front_pos):
     *pieces, share, chunk = prep(
         block_of_slot,
@@ -214,28 +254,17 @@
         sigma_hist.reshape(128, 128),
         diag_inv,
     )
-    rows = [pieces[0]]
-    for d in (2, 1, 3):
-        pairs = [(ring_index(y), ring_index((y + d) % 4)) for y in range(4)]
-        rows.append(lax.ppermute(pieces[d], RING, pairs))
-    rows = [rows[0], rows[2], rows[1], rows[3]]
-    shares = lax.all_gather(share, "core")
-    message = pl.pallas_call(
-        along_z_kernel,
-        in_specs=[whole(), whole()],
-        out_specs=whole(),
-        out_shape=jax.ShapeDtypeStruct((16, 96, 128), BF16),
-        name="along_z",
-    )(shares, chunk)
-    message = lax.all_to_all(message, "z", 0, 0, tiled=True)
-    message = pl.pallas_call(
-        along_x_kernel,
-        in_specs=[whole()],
-        out_specs=whole(),
-        out_shape=jax.ShapeDtypeStruct((4, 1056, 128), BF16),
-        name="along_x",
-    )(message)
-    mine = lax.all_to_all(message, "x", 0, 0, tiled=True)
+    opposite = along_ring(pieces[2], 2)
+    mine, before, after = lax.cond(
+        front_pos[0] >= 0,
+        gathered,
+        lambda share, chunk, *near_pieces: (jnp.zeros((4, 1056, 128), BF16), *near_pieces),
+        share,
+        chunk,
+        pieces[1],
+        pieces[3],
+    )
+    rows = [pieces[0], before, opposite, after]
     other = lax.ppermute(mine, "core", [(0, 1), (1, 0)])
     part = dots(mine, rows, 0)
     tail = pl.BlockSpec((4, SPLIT_ROWS, 128), lambda i: (0, 1024 // SPLIT_ROWS, 0))
@@ -261,8 +290,9 @@
         in_specs=[whole()],
         out_specs=(whole(), whole()),
         out_shape=(out, out),
+        compiler_params=ROOM,
         name="last",
-    )(sums)
+    )(near(sums))
 
 
 def solution(mesh):

time: 104 us -> 90.6 us (0.87)
  the two profiles are of different devices: /device:TPU:1 before, /device:TPU:32 now
where the time goes in v3:
time: 90.6 us; the launch traced here: 90 us
  starting transfers between devices  33.5 us (37%)
  waiting for transfers between devices  25.5 us (28%)
  Pallas kernels  13.1 us (14%)
  blocking collectives  12.5 us (14%)
  local copies, waits for them, and re-layouts  4.57 us (5%)
    all_to_all x1, starting transfers between devices, gathered(): message = lax.all_to_all(message, 'z', 0, 0, tiled=True)  15.2 us
    all_to_all x1, waiting for transfers between devices, gathered(): message = lax.all_to_all(message, 'z', 0, 0, tiled=True)  15.2 us
    ppermute x3, starting transfers between devices, along_ring(): lax.ppermute(piece, RING, [(ring_index(y), ring_index((y + d) % 4)) for y...  12.1 us
    all_to_all x1, blocking collectives, body(): sums = lax.all_to_all(sums, RING, 0, 0, tiled=True)  10.5 us
    all_to_all x1, waiting for transfers between devices, gathered(): return (lax.all_to_all(message, 'x', 0, 0, tiled=True), first, third)  9.73 us
    pallas_call x2, Pallas kernels, dots(): pl.pallas_call(kernel, grid=(4,), in_specs=[pl.BlockSpec((1, 1056, 128),...  5.37 us
    pallas_call x1, Pallas kernels, prep(): pl.pallas_call(prep_kernel, grid=(8 // PAIRS,), in_specs=[whole(SMEM), wh...  4.78 us
    cond x4, local copies, waits for them, and re-layouts  4.55 us
  transfers between devices with their start and end apart: 6, of which 3 were waited for; matrix products, arithmetic and copies ran while one was open for 5% of the time, Pallas kernels for 6%

profile of v3, /device:TPU:32, one launch (start us, length us, event | category | flops | bytes accessed | tf_op | source)
XLA Modules:
  0.0 90.0 jit_solution(9265730760049790508)
XLA Ops:
  0.6 0.0 copy-start.5
  0.6 4.8 %prep.1 = (bf16[8,64,1024]{2,1,0:T(8,128)(2,1)}, bf16[8,64,1024]{2,1,0:T(8,128)(2,1)}, bf16[8,64,1024]{2,1,0:T(8,128)(2,1)}, bf16[8,64,1024]{2,1,0:T(8,128)(2,1)...) custom-call(s32[256]{0:T(256)} %slots.1, s32[2]{0:T(128)} %fronts.1, bf16[64,32768]{1,0:T(8,128)(2,1)} %bitcast.8, ...), custom_call_target="tpu_custom_call" | custom-call | tf_op jit(solution)/shard_map/prep/pallas_call | solution.py:93
  5.4 5.1 %collective-permute-start.3 = (bf16[8,64,1024]{2,1,0:T(8,128)(2,1)}, bf16[8,64,1024]{2,1,0:T(8,128)(2,1)S(1)}, u32[]{:S(2)}, u32[]{:S(2)}) collective-permute-start(bf16[8,64,1024]{2,1,0:T(8,128)(2,1)} %get-tuple-element.36), channel_id=1, source_target_pairs={{0,1},{4,5},{1,0},{5,4},{2,3},{6,7},{3,2},{7,6},{8,9},{12,13},{9,8... | collective-permute-start | bytes 3145736 | tf_op jit(solution)/shard_map/ppermute | solution.py:223
  10.5 0.0 copy-done.5
  10.6 0.0 copy-start
  10.6 60.5 %conditional.1 = (bf16[4,1056,128]{2,1,0:T(8,128)(2,1)}, bf16[8,64,1024]{2,1,0:T(8,128)(2,1)}, bf16[8,64,1024]{2,1,0:T(8,128)(2,1)}) conditional(s32[]{:T(128)} %bitcast.1, (bf16[8,64,1024]{2,1,0:T(8,128)(2,1)}, bf16[8,64,1024]{2,1,0:T(8,128)(2,1)}) %tuple.15, (f32[32,128]{1,0:T(8,128)S(1)}, bf16[64,128]{1,0:T(8,128)(2,1)S(1)}, ...), branch_computations={%region_0.0_spmd, %region_1.0_spmd} | conditional | bytes 21250244 | solution.py:258
  10.6 2.0 %all-gather = f32[64,128]{1,0:T(8,128)S(1)} all-gather(f32[32,128]{1,0:T(8,128)S(1)} %get-tuple-element.14), channel_id=2, replica_groups=mesh['z'=16,'x'=4,'yl'=2,'core'=2,'yh'=2] {'core'}, dimensions={0}, use_global_device_ids=true | all-gather | bytes 49152 | tf_op jit(solution)/shard_map/cond/branch_1_fun/all_gather | solution.py:227
  12.6 0.0 copy-start.2
  12.6 0.8 along_z.1
  13.4 15.2 %all-to-all-start = ((bf16[16,96,128]{2,1,0:T(8,128)(2,1)}), bf16[16,96,128]{2,1,0:T(8,128)(2,1)S(1)}, u32[]{:S(2)}, u32[]{:S(2)}) async-start(bf16[16,96,128]{2,1,0:T(8,128)(2,1)} %along_z.1), calls=%async_computation | async-start | bytes 786432 | tf_op jit(solution)/shard_map/cond/branch_1_fun/all_to_all | solution.py:236
  28.6 2.6 %collective-permute-start = (bf16[8,64,1024]{2,1,0:T(8,128)(2,1)}, bf16[8,64,1024]{2,1,0:T(8,128)(2,1)}, u32[]{:S(2)}, u32[]{:S(2)}) collective-permute-start(bf16[8,64,1024]{2,1,0:T(8,128)(2,1)} %get-tuple-element.16), channel_id=1, source_target_pairs={{0,4},{4,1},{1,5},{5,0},{2,6},{6,3},{3,7},{7,2},{8,12},{12,9},{9,1... | collective-permute-start | bytes 3145736 | tf_op jit(solution)/shard_map/cond/branch_1_fun/ppermute | solution.py:223
  31.2 0.0 copy-done.2
  31.2 4.5 %collective-permute-start.1 = (bf16[8,64,1024]{2,1,0:T(8,128)(2,1)S(1)}, bf16[8,64,1024]{2,1,0:T(8,128)(2,1)}, u32[]{:S(2)}, u32[]{:S(2)}) collective-permute-start(bf16[8,64,1024]{2,1,0:T(8,128)(2,1)S(1)} %copy-done.2), channel_id=1, source_target_pairs={{0,5},{4,0},{1,4},{5,1},{2,7},{6,2},{3,6},{7,3},{8,13},{12,8},{9,1... | collective-permute-start | bytes 3145736 | tf_op jit(solution)/shard_map/cond/branch_1_fun/ppermute | solution.py:223
  35.6 15.2 %all-to-all-done.in_ref = bf16[16,96,128]{2,1,0:T(8,128)(2,1)S(1)} async-done(((bf16[16,96,128]{2,1,0:T(8,128)(2,1)}), bf16[16,96,128]{2,1,0:T(8,128)(2,1)S(1)}, u32[]{:S(2)}, u32[]{:S(2)}) %all-to-all-start) | async-done | bytes 393248 | tf_op jit(solution)/shard_map/cond/branch_1_fun/all_to_all | solution.py:236
  50.8 1.1 %along_x.1 = bf16[4,1056,128]{2,1,0:T(8,128)(2,1)} custom-call(bf16[16,96,128]{2,1,0:T(8,128)(2,1)S(1)} %all-to-all-done.in_ref), custom_call_target="tpu_custom_call" | custom-call | tf_op jit(solution)/shard_map/cond/branch_1_fun/along_x/pallas_call | solution.py:237
  52.0 4.3 %all-to-all-start.1 = ((bf16[4,1056,128]{2,1,0:T(8,128)(2,1)}), bf16[4,1056,128]{2,1,0:T(8,128)(2,1)}, u32[]{:S(2)}, u32[]{:S(2)}) async-start(bf16[4,1056,128]{2,1,0:T(8,128)(2,1)} %along_x.1), calls=%async_computation.1 | async-start | bytes 2162688 | tf_op jit(solution)/shard_map/cond/branch_1_fun/all_to_all | solution.py:246
  56.3 0.6 collective-permute-done
  56.8 2.3 %copy.12 = bf16[8,64,1024]{2,1,0:T(8,128)(2,1)} copy(bf16[8,64,1024]{2,1,0:T(8,128)(2,1)} %collective-permute-done) | data formatting | bytes 2097152 | tf_op jit(solution)/shard_map/cond
  59.1 0.0 collective-permute-done.1
  59.1 2.3 %copy.13 = bf16[8,64,1024]{2,1,0:T(8,128)(2,1)} copy(bf16[8,64,1024]{2,1,0:T(8,128)(2,1)} %collective-permute-done.1) | data formatting | bytes 2097152 | tf_op jit(solution)/shard_map/cond
  61.4 9.7 %all-to-all-done.1 = bf16[4,1056,128]{2,1,0:T(8,128)(2,1)} async-done(((bf16[4,1056,128]{2,1,0:T(8,128)(2,1)}), bf16[4,1056,128]{2,1,0:T(8,128)(2,1)}, u32[]{:S(2)}, u32[]{:S(2)}) %all-to-all-start.1) | async-done | bytes 1081376 | tf_op jit(solution)/shard_map/cond/branch_1_fun/all_to_all | solution.py:246
  71.1 1.9 %collective-permute-start.2 = (bf16[4,1056,128]{2,1,0:T(8,128)(2,1)}, bf16[4,1056,128]{2,1,0:T(8,128)(2,1)S(1)}, u32[]{:S(2)}, u32[]{:S(2)}) collective-permute-start(bf16[4,1056,128]{2,1,0:T(8,128)(2,1)} %get-tuple-element.33.s_ref.mine_ref), channel_id=1, source_target_pairs={{0,2},{2,0},{1,3},{3,1},{4,6},{6,4},{5,7},{7,5},{8,10},{10,8},{9,1... | collective-permute-start | bytes 3244040 | tf_op jit(solution)/shard_map/ppermute | solution.py:268
  73.0 0.0 collective-permute-done.3.g2
  73.0 0.0 copy-done
  73.0 0.0 copy-start.1
  73.1 0.0 copy-start.3
  73.1 0.0 copy-start.4
  73.1 3.2 %first_kernel.1 = f32[256,128]{1,0:T(8,128)S(1)} custom-call(bf16[4,1056,128]{2,1,0:T(8,128)(2,1)} %get-tuple-element.33.s_ref.mine_ref, bf16[8,64,1024]{2,1,0:T(8,128)(2,1)S(1)} %copy-done, bf16[8,64,1024]{2,1,0:T(8,128)(2,1)} %get-tuple-element.35.g1, bf16[8,64,1024]{2,1,0:T(8,128)(2,1)S(1)} %collective-permute-done.3.g2, ...), custom_call_target="tpu_custom_call" | custom-call | flops 32212254720 | bytes 3145728 | tf_op jit(solution)/shard_map/first_kernel/pallas_call | solution.py:183
  76.3 0.0 collective-permute-done.2.s_ref.other_ref
  76.3 0.0 copy-done.1
  76.3 0.0 copy-done.3
  76.3 0.0 copy-done.4
  76.3 2.2 %second_kernel.1 = f32[4,160,128]{2,1,0:T(8,128)S(1)} custom-call(bf16[4,1056,128]{2,1,0:T(8,128)(2,1)S(1)} %collective-permute-done.2.s_ref.other_ref, bf16[8,64,1024]{2,1,0:T(8,128)(2,1)S(1)} %copy-done, bf16[8,64,1024]{2,1,0:T(8,128)(2,1)S(1)} %copy-done.4, bf16[8,64,1024]{2,1,0:T(8,128)(2,1)S(1)} %collective-permute-done.3.g2, ...), custom_call_target="tpu_custom_call" | custom-call | flops 268435456 | bytes 3145728 | tf_op jit(solution)/shard_map/second_kernel/pallas_call | solution.py:183
  78.5 10.5 %all_to_all.13.in_ref = f32[4,160,128]{2,1,0:T(8,128)S(1)} all-to-all(f32[4,160,128]{2,1,0:T(8,128)S(1)} %second_kernel.1), channel_id=1, replica_groups=mesh['z'=16,'x'=4,'yl'=2,'core'=2,'yh'=2] {'yl','yh'}, dimensions={0} | all-to-all | bytes 655360 | tf_op jit(solution)/shard_map/all_to_all | solution.py:286
  89.0 1.0 %last.1 = (f32[2,2,32,64]{3,2,1,0:T(8,128)}, f32[2,2,32,64]{3,2,1,0:T(8,128)}) custom-call(f32[4,160,128]{2,1,0:T(8,128)S(1)} %all_to_all.13.in_ref), custom_call_target="tpu_custom_call" | custom-call | tf_op jit(solution)/shard_map/last/pallas_call | solution.py:288
Async XLA Ops:
  0.6 9.9 %copy-start.5 = (s32[2]{0:T(128)S(1)}, s32[2]{0:T(128)}, u32[]{:S(2)}) copy-start(s32[2]{0:T(128)} %fronts.1) | copy-start | bytes 28
  5.4 67.6 %collective-permute-start.3 = (bf16[8,64,1024]{2,1,0:T(8,128)(2,1)}, bf16[8,64,1024]{2,1,0:T(8,128)(2,1)S(1)}, u32[]{:S(2)}, u32[]{:S(2)}) collective-permute-start(bf16[8,64,1024]{2,1,0:T(8,128)(2,1)} %get-tuple-element.36), channel_id=1, source_target_pairs={{0,1},{4,5},{1,0},{5,4},{2,3},{6,7},{3,2},{7,6},{8,9},{12,13},{9,8... | collective-permute-start | bytes 3145736 | tf_op jit(solution)/shard_map/ppermute | solution.py:223
  10.6 62.5 %copy-start = (bf16[8,64,1024]{2,1,0:T(8,128)(2,1)S(1)}, bf16[8,64,1024]{2,1,0:T(8,128)(2,1)}, u32[]{:S(2)}) copy-start(bf16[8,64,1024]{2,1,0:T(8,128)(2,1)} %get-tuple-element.34.g0) | copy-start | bytes 3145732
  12.6 18.6 %copy-start.2 = (bf16[8,64,1024]{2,1,0:T(8,128)(2,1)S(1)}, bf16[8,64,1024]{2,1,0:T(8,128)(2,1)}, u32[]{:S(2)}) copy-start(bf16[8,64,1024]{2,1,0:T(8,128)(2,1)} %get-tuple-element.17) | copy-start | bytes 3145732 | tf_op jit(solution)/shard_map/cond
  13.4 37.5 %all-to-all-start = ((bf16[16,96,128]{2,1,0:T(8,128)(2,1)}), bf16[16,96,128]{2,1,0:T(8,128)(2,1)S(1)}, u32[]{:S(2)}, u32[]{:S(2)}) async-start(bf16[16,96,128]{2,1,0:T(8,128)(2,1)} %along_z.1), calls=%async_computation | async-start | bytes 786432 | tf_op jit(solution)/shard_map/cond/branch_1_fun/all_to_all | solution.py:236
  28.6 28.3 %collective-permute-start = (bf16[8,64,1024]{2,1,0:T(8,128)(2,1)}, bf16[8,64,1024]{2,1,0:T(8,128)(2,1)}, u32[]{:S(2)}, u32[]{:S(2)}) collective-permute-start(bf16[8,64,1024]{2,1,0:T(8,128)(2,1)} %get-tuple-element.16), channel_id=1, source_target_pairs={{0,4},{4,1},{1,5},{5,0},{2,6},{6,3},{3,7},{7,2},{8,12},{12,9},{9,1... | collective-permute-start | bytes 3145736 | tf_op jit(solution)/shard_map/cond/branch_1_fun/ppermute | solution.py:223
  31.2 27.9 %collective-permute-start.1 = (bf16[8,64,1024]{2,1,0:T(8,128)(2,1)S(1)}, bf16[8,64,1024]{2,1,0:T(8,128)(2,1)}, u32[]{:S(2)}, u32[]{:S(2)}) collective-permute-start(bf16[8,64,1024]{2,1,0:T(8,128)(2,1)S(1)} %copy-done.2), channel_id=1, source_target_pairs={{0,5},{4,0},{1,4},{5,1},{2,7},{6,2},{3,6},{7,3},{8,13},{12,8},{9,1... | collective-permute-start | bytes 3145736 | tf_op jit(solution)/shard_map/cond/branch_1_fun/ppermute | solution.py:223
  52.0 19.1 %all-to-all-start.1 = ((bf16[4,1056,128]{2,1,0:T(8,128)(2,1)}), bf16[4,1056,128]{2,1,0:T(8,128)(2,1)}, u32[]{:S(2)}, u32[]{:S(2)}) async-start(bf16[4,1056,128]{2,1,0:T(8,128)(2,1)} %along_x.1), calls=%async_computation.1 | async-start | bytes 2162688 | tf_op jit(solution)/shard_map/cond/branch_1_fun/all_to_all | solution.py:246
  71.1 5.2 %collective-permute-start.2 = (bf16[4,1056,128]{2,1,0:T(8,128)(2,1)}, bf16[4,1056,128]{2,1,0:T(8,128)(2,1)S(1)}, u32[]{:S(2)}, u32[]{:S(2)}) collective-permute-start(bf16[4,1056,128]{2,1,0:T(8,128)(2,1)} %get-tuple-element.33.s_ref.mine_ref), channel_id=1, source_target_pairs={{0,2},{2,0},{1,3},{3,1},{4,6},{6,4},{5,7},{7,5},{8,10},{10,8},{9,1... | collective-permute-start | bytes 3244040 | tf_op jit(solution)/shard_map/ppermute | solution.py:268
  73.0 3.3 %copy-start.1 = (f32[2,2,32,64]{3,2,1,0:T(8,128)S(1)}, f32[2,2,32,64]{3,2,1,0:T(8,128)}, u32[]{:S(2)}) copy-start(f32[2,2,32,64]{3,2,1,0:T(8,128)} %prev_ref.1) | copy-start | bytes 98308
  73.1 3.3 %copy-start.3 = (bf16[8,64,1024]{2,1,0:T(8,128)(2,1)S(1)}, bf16[8,64,1024]{2,1,0:T(8,128)(2,1)}, u32[]{:S(2)}) copy-start(bf16[8,64,1024]{2,1,0:T(8,128)(2,1)} %get-tuple-element.37.g3) | copy-start | bytes 3145732
  73.1 3.3 %copy-start.4 = (bf16[8,64,1024]{2,1,0:T(8,128)(2,1)S(1)}, bf16[8,64,1024]{2,1,0:T(8,128)(2,1)}, u32[]{:S(2)}) copy-start(bf16[8,64,1024]{2,1,0:T(8,128)(2,1)} %get-tuple-element.35.g1) | copy-start | bytes 3145732

commit v4 on v3

--- a/solution.py
+++ b/solution.py
@@ -36,8 +36,7 @@
     return (y % 2) * 2 + y // 2
 
 
-def prep_kernel(slots, fronts, g_ref, sigma_ref, inv_ref, *outs):
-    piece_refs, share_ref, chunk_ref = outs[:4], outs[4], outs[5]
+def sort_pieces(slots, g_ref, near_refs, far_refs):
     step = pl.program_id(0)
     yl, core, yh = lax.axis_index("yl"), lax.axis_index("core"), lax.axis_index("yh")
     hist = ((lax.axis_index("z") * 4 + lax.axis_index("x")) * 2 + yl) * 2 + core
@@ -46,12 +45,16 @@
     row = lax.broadcasted_iota(jnp.int32, (64, 128), 0)
     upper = (lane >= 64).astype(jnp.int32)
     ahead = upper * 32 - first - (row >= 32).astype(jnp.int32)
-    pick_in = lax.broadcasted_iota(jnp.int32, (256, 256), 0)
-    pick_out = lax.broadcasted_iota(jnp.int32, (256, 256), 1)
-    for d in range(2):
+    for d, refs in enumerate(zip(near_refs, far_refs, strict=True)):
         y = (yh * 2 + yl + d) % 4
-        to_yl, to_yh = y % 2, y // 2
-        half = jnp.where(pick_out < 128, to_yh, 1 - to_yh)
+        to_yl = y % 2
+        ends = [(ref, y // 2 if far == 0 else 1 - y // 2) for far, ref in enumerate(refs) if ref is not None]
+        if not ends:
+            continue
+        width = 128 * len(ends)
+        pick_in = lax.broadcasted_iota(jnp.int32, (256, width), 0)
+        pick_out = lax.broadcasted_iota(jnp.int32, (256, width), 1)
+        half = jnp.where(pick_out < 128, ends[0][1], ends[-1][1])
         within = pick_out % 128
         pick = pick_in == within + 64 * (within >= 64).astype(jnp.int32) + 64 * half
         pick = jnp.where(pick, 1.0, 0.0).astype(BF16)
@@ -70,17 +73,25 @@
                 for x in range(4):
                     at = h * 4 + x
                     term = (step * PAIRS + p) * 64 + x * 8 + to_yl * 4 + to_core * 2
-                    for far in range(2):
-                        e = 1 - to_yh if far else to_yh
-                        block = picked[at * 64 : at * 64 + 64, far * 128 : far * 128 + 128]
+                    for n, (ref, e) in enumerate(ends):
+                        block = picked[at * 64 : at * 64 + 64, n * 128 : n * 128 + 128]
                         block = jnp.where(ahead + (term + e) >= 0, block, 0.0)
-                        piece_refs[d + 2 * far][at, :, p * 128 : p * 128 + 128] = block.astype(BF16)
-
-    @pl.when(step == 0)
-    def _():
+                        ref[at, :, p * 128 : p * 128 + 128] = block.astype(BF16)
+
+
+def opposite_kernel(slots, fronts, g_ref, sigma_ref, inv_ref, piece_ref, share_ref, chunk_ref):
+    sort_pieces(slots, g_ref, (None,), (piece_ref,))
+
+    @pl.when(pl.program_id(0) == 0)
+    def _():
+        yh = lax.axis_index("yh")
+        hist = 0
+        for axis, size in zip(HIST, (16, 4, 2, 2), strict=True):
+            hist = hist * size + lax.axis_index(axis)
+        lane = lax.broadcasted_iota(jnp.int32, (64, 128), 1)
         flipped = sigma_ref[...].astype(F32).T
         mine = jnp.where(yh == 0, flipped[:64], flipped[64:])
-        limit = jnp.where(upper > 0, fronts[1], fronts[0])
+        limit = jnp.where(lane >= 64, fronts[1], fronts[0])
         chunk_ref[...] = jnp.where(2 * hist + yh <= limit, mine, 0.0).astype(BF16)
         when = jnp.where(yh == 0, fronts[0], fronts[1])
         block = jnp.where(when % 2 == 0, inv_ref[0], inv_ref[1])
@@ -89,24 +100,45 @@
         share_ref[:, 64:] = block[32:]
 
 
-def prep(slots, fronts, g_hist, sigma_hist, diag_inv):
+def others_kernel(slots, g_ref, own_ref, first_ref, third_ref):
+    sort_pieces(slots, g_ref, (own_ref, first_ref), (None, third_ref))
+
+
+G_SPEC = pl.BlockSpec((64, 4096 * PAIRS), lambda i: (0, i))
+PIECE_SPEC = pl.BlockSpec((8, 64, 128 * PAIRS), lambda i: (0, 0, i))
+PIECE = pltpu.HBM((8, 64, 1024), BF16)
+
+
+def prep_opposite(slots, fronts, g_hist, sigma_hist, diag_inv):
     return pl.pallas_call(
-        prep_kernel,
+        opposite_kernel,
         grid=(8 // PAIRS,),
         in_specs=[
             whole(SMEM),
             whole(SMEM),
-            pl.BlockSpec((64, 4096 * PAIRS), lambda i: (0, i)),
+            G_SPEC,
             pl.BlockSpec((128, 128), lambda i: (0, 0)),
             pl.BlockSpec((2, 64, 64), lambda i: (0, 0, 0)),
         ],
-        out_specs=[pl.BlockSpec((8, 64, 128 * PAIRS), lambda i: (0, 0, i))] * 4
+        out_specs=[PIECE_SPEC]
         + [pl.BlockSpec((32, 128), lambda i: (0, 0)), pl.BlockSpec((64, 128), lambda i: (0, 0))],
-        out_shape=[pltpu.HBM((8, 64, 1024), BF16)] * 4
-        + [VMEM((32, 128), F32), VMEM((64, 128), BF16)],
-        compiler_params=ROOM,
-        name="prep",
+        out_shape=[PIECE] + [VMEM((32, 128), F32), VMEM((64, 128), BF16)],
+        compiler_params=ROOM,
+        name="prep_opposite",
     )(far(slots), far(fronts), far(g_hist), far(sigma_hist), far(diag_inv))
+
+
+def prep_others(slots, g_hist):
+    return pl.pallas_call(
+        others_kernel,
+        grid=(8 // PAIRS,),
+        in_specs=[whole(SMEM), G_SPEC],
+        out_specs=[PIECE_SPEC] * 3,
+        out_shape=[PIECE] * 3,
+        compiler_params=ROOM,
+        cost_estimate=pl.CostEstimate(flops=1 << 29, bytes_accessed=6 << 20, transcendentals=0),
+        name="prep_others",
+    )(far(slots), far(g_hist))
 
 
 def along_z_kernel(shares_ref, chunk_ref, out_ref):
@@ -223,7 +255,9 @@
     return lax.ppermute(piece, RING, [(ring_index(y), ring_index((y + d) % 4)) for y in range(4)])
 
 
-def gathered(share, chunk, first, third):
+def gathered(share, chunk, slots, g_hist):
+    own, first, third = prep_others(slots, g_hist)
+    first, third = along_ring(first, 1), along_ring(third, 3)
     shares = lax.all_gather(share, "core")
     message = pl.pallas_call(
         along_z_kernel,
@@ -242,29 +276,25 @@
         compiler_params=ROOM,
         name="along_x",
     )(near(message))
-    first, third = along_ring(first, 1), along_ring(third, 3)
-    return lax.all_to_all(message, "x", 0, 0, tiled=True), first, third
+    return lax.all_to_all(message, "x", 0, 0, tiled=True), own, first, third
 
 
 def body(g_hist, sigma_hist, diag_inv, previous, block_of_slot, front_pos):
-    *pieces, share, chunk = prep(
-        block_of_slot,
-        front_pos,
-        g_hist.reshape(64, 32768),
-        sigma_hist.reshape(128, 128),
-        diag_inv,
+    g_hist = g_hist.reshape(64, 32768)
+    opposite, share, chunk = prep_opposite(
+        block_of_slot, front_pos, g_hist, sigma_hist.reshape(128, 128), diag_inv
     )
-    opposite = along_ring(pieces[2], 2)
-    mine, before, after = lax.cond(
+    opposite = along_ring(opposite, 2)
+    mine, own, before, after = lax.cond(
         front_pos[0] >= 0,
         gathered,
-        lambda share, chunk, *near_pieces: (jnp.zeros((4, 1056, 128), BF16), *near_pieces),
+        lambda *_: tuple(jnp.zeros(n, BF16) for n in ((4, 1056, 128), *[opposite.shape] * 3)),
         share,
         chunk,
-        pieces[1],
-        pieces[3],
+        block_of_slot,
+        g_hist,
     )
-    rows = [pieces[0], before, opposite, after]
+    rows = [own, before, opposite, after]
     other = lax.ppermute(mine, "core", [(0, 1), (1, 0)])
     part = dots(mine, rows, 0)
     tail = pl.BlockSpec((4, SPLIT_ROWS, 128), lambda i: (0, 1024 // SPLIT_ROWS, 0))

time: 90.6 us -> 90.2 us (level)
  local copies, waits for them, and re-layouts: 4.57 us -> 0.01 us
  Pallas kernels: 13.1 us -> 17.1 us
    ppermute x3, waiting for transfers between devices: 0.56 us -> 5.79 us  [along_ring(): lax.ppermute(piece, RING, [(ring_index(y), ring_index((y + d) % 4)) for y...]
    cond x4 -> x2, local copies, waits for them, and re-layouts: 4.55 us -> 0.01 us
    all_to_all x1, waiting for transfers between devices: 15.2 us -> 10.9 us  [gathered(): message = lax.all_to_all(message, 'z', 0, 0, tiled=True)]
    pallas_call x1 -> x2, Pallas kernels: 4.78 us -> 7.99 us  [the longest x1 4.34 us: prep_others(): pl.pallas_call(others_kernel, grid=(8 // PAIRS,), in_specs=[whole(SMEM),...]
  transfers between devices with their start and end apart: 6 -> 6, of which waited for: 3 -> 4; matrix products, arithmetic and copies ran while one was open for 5% -> 0% of each run, Pallas kernels for 6% -> 10%
where the time goes in v4:
time: 90.2 us; the launch traced here: 89.6 us
  starting transfers between devices  33.7 us (37%)
  waiting for transfers between devices  25.7 us (28%)
  Pallas kernels  17.1 us (19%)
  blocking collectives  12.3 us (14%)
    all_to_all x1, starting transfers between devices, gathered(): message = lax.all_to_all(message, 'z', 0, 0, tiled=True)  15.2 us
    ppermute x3, starting transfers between devices, along_ring(): lax.ppermute(piece, RING, [(ring_index(y), ring_index((y + d) % 4)) for y...  12.1 us
    all_to_all x1, waiting for transfers between devices, gathered(): message = lax.all_to_all(message, 'z', 0, 0, tiled=True)  10.9 us
    all_to_all x1, blocking collectives, body(): sums = lax.all_to_all(sums, RING, 0, 0, tiled=True)  10.5 us
    all_to_all x1, waiting for transfers between devices, gathered(): return (lax.all_to_all(message, 'x', 0, 0, tiled=True), own, first, third)  9.06 us
    pallas_call x2, Pallas kernels, dots(): pl.pallas_call(kernel, grid=(4,), in_specs=[pl.BlockSpec((1, 1056, 128),...  6.17 us
    ppermute x3, waiting for transfers between devices, along_ring(): lax.ppermute(piece, RING, [(ring_index(y), ring_index((y + d) % 4)) for y...  5.79 us
    all_to_all x1, starting transfers between devices, gathered(): return (lax.all_to_all(message, 'x', 0, 0, tiled=True), own, first, third)  4.42 us
  transfers between devices with their start and end apart: 6, of which 4 were waited for; matrix products, arithmetic and copies ran while one was open for 0% of the time, Pallas kernels for 10%

profile of v4, /device:TPU:32, one launch (start us, length us, event | category | flops | bytes accessed | tf_op | source)
XLA Modules:
  0.0 89.6 jit_solution(7842830311432182833)
XLA Ops:
  0.6 0.0 copy-start.2
  0.6 3.6 %prep_opposite.1 = (bf16[8,64,1024]{2,1,0:T(8,128)(2,1)}, f32[32,128]{1,0:T(8,128)S(1)}, bf16[64,128]{1,0:T(8,128)(2,1)S(1)}) custom-call(s32[256]{0:T(256)} %slots.1, s32[2]{0:T(128)} %fronts.1, bf16[64,32768]{1,0:T(8,128)(2,1)} %bitcast.8, bf16[128,128]{1,0:T(8,128)(2,1)} %bitcast.10, f32[2,64,64]{2,1,0:T(8,128)} %inv_ref.1), custom_call_target="tpu_custom_call" | custom-call | tf_op jit(solution)/shard_map/prep_opposite/pallas_call | solution.py:113
  4.3 5.1 %collective-permute-start.3 = (bf16[8,64,1024]{2,1,0:T(8,128)(2,1)}, bf16[8,64,1024]{2,1,0:T(8,128)(2,1)S(1)}, u32[]{:S(2)}, u32[]{:S(2)}) collective-permute-start(bf16[8,64,1024]{2,1,0:T(8,128)(2,1)} %get-tuple-element.29), channel_id=1, source_target_pairs={{0,1},{4,5},{1,0},{5,4},{2,3},{6,7},{3,2},{7,6},{8,9},{12,13},{9,8... | collective-permute-start | bytes 3145736 | tf_op jit(solution)/shard_map/ppermute | solution.py:255
  9.4 0.0 copy-done.2
  9.4 60.5 %conditional.1 = (bf16[4,1056,128]{2,1,0:T(8,128)(2,1)}, bf16[8,64,1024]{2,1,0:T(8,128)(2,1)S(1)}, bf16[8,64,1024]{2,1,0:T(8,128)(2,1)}, bf16[8,64,1024]{2,1,0:T(8,128)(2,1)}) conditional(s32[]{:T(128)} %bitcast.1, () %tuple.15, (f32[32,128]{1,0:T(8,128)S(1)}, bf16[64,128]{1,0:T(8,128)(2,1)S(1)}, s32[256]{0:T(256)}, bf16[64,32768]{1,0:T(8,128)(2,1)}) %tuple.19), branch_computations={%region_0.0_spmd, %region_1.0_spmd} | conditional | flops 536870912 | bytes 23347404 | solution.py:288
  9.4 1.8 %all-gather = f32[64,128]{1,0:T(8,128)S(1)} all-gather(f32[32,128]{1,0:T(8,128)S(1)} %get-tuple-element.8), channel_id=2, replica_groups=mesh['z'=16,'x'=4,'yl'=2,'core'=2,'yh'=2] {'core'}, dimensions={0}, use_global_device_ids=true | all-gather | bytes 49152 | tf_op jit(solution)/shard_map/cond/branch_1_fun/all_gather | solution.py:261
  11.3 0.8 along_z.1
  12.1 15.2 %all-to-all-start = ((bf16[16,96,128]{2,1,0:T(8,128)(2,1)}), bf16[16,96,128]{2,1,0:T(8,128)(2,1)S(1)}, u32[]{:S(2)}, u32[]{:S(2)}) async-start(bf16[16,96,128]{2,1,0:T(8,128)(2,1)} %along_z.1), calls=%async_computation | async-start | bytes 786432 | tf_op jit(solution)/shard_map/cond/branch_1_fun/all_to_all | solution.py:270
  27.3 4.3 %prep_others.1 = (bf16[8,64,1024]{2,1,0:T(8,128)(2,1)}, bf16[8,64,1024]{2,1,0:T(8,128)(2,1)}, bf16[8,64,1024]{2,1,0:T(8,128)(2,1)}) custom-call(s32[256]{0:T(256)} %get-tuple-element.10.slots, bf16[64,32768]{1,0:T(8,128)(2,1)} %get-tuple-element.11.g_ref), custom_call_target="tpu_custom_call" | custom-call | flops 536870912 | bytes 6291456 | tf_op jit(solution)/shard_map/cond/branch_1_fun/prep_others/pallas_call | solution.py:132
  31.6 2.6 %collective-permute-start = (bf16[8,64,1024]{2,1,0:T(8,128)(2,1)}, bf16[8,64,1024]{2,1,0:T(8,128)(2,1)}, u32[]{:S(2)}, u32[]{:S(2)}) collective-permute-start(bf16[8,64,1024]{2,1,0:T(8,128)(2,1)} %get-tuple-element.13), channel_id=1, source_target_pairs={{0,4},{4,1},{1,5},{5,0},{2,6},{6,3},{3,7},{7,2},{8,12},{12,9},{9,1... | collective-permute-start | bytes 3145736 | tf_op jit(solution)/shard_map/cond/branch_1_fun/ppermute | solution.py:255
  34.2 4.5 %collective-permute-start.1 = (bf16[8,64,1024]{2,1,0:T(8,128)(2,1)}, bf16[8,64,1024]{2,1,0:T(8,128)(2,1)}, u32[]{:S(2)}, u32[]{:S(2)}) collective-permute-start(bf16[8,64,1024]{2,1,0:T(8,128)(2,1)} %get-tuple-element.14), channel_id=1, source_target_pairs={{0,5},{4,0},{1,4},{5,1},{2,7},{6,2},{3,6},{7,3},{8,13},{12,8},{9,1... | collective-permute-start | bytes 3145736 | tf_op jit(solution)/shard_map/cond/branch_1_fun/ppermute | solution.py:255
  38.7 10.9 %all-to-all-done.in_ref = bf16[16,96,128]{2,1,0:T(8,128)(2,1)S(1)} async-done(((bf16[16,96,128]{2,1,0:T(8,128)(2,1)}), bf16[16,96,128]{2,1,0:T(8,128)(2,1)S(1)}, u32[]{:S(2)}, u32[]{:S(2)}) %all-to-all-start) | async-done | bytes 393248 | tf_op jit(solution)/shard_map/cond/branch_1_fun/all_to_all | solution.py:270
  49.5 1.1 %along_x.1 = bf16[4,1056,128]{2,1,0:T(8,128)(2,1)} custom-call(bf16[16,96,128]{2,1,0:T(8,128)(2,1)S(1)} %all-to-all-done.in_ref), custom_call_target="tpu_custom_call" | custom-call | tf_op jit(solution)/shard_map/cond/branch_1_fun/along_x/pallas_call | solution.py:271
  50.7 0.0 copy-start.1
  50.7 4.4 %all-to-all-start.1 = ((bf16[4,1056,128]{2,1,0:T(8,128)(2,1)}), bf16[4,1056,128]{2,1,0:T(8,128)(2,1)}, u32[]{:S(2)}, u32[]{:S(2)}) async-start(bf16[4,1056,128]{2,1,0:T(8,128)(2,1)} %along_x.1), calls=%async_computation.1 | async-start | bytes 2162688 | tf_op jit(solution)/shard_map/cond/branch_1_fun/all_to_all | solution.py:279
  55.1 4.6 %collective-permute-done = bf16[8,64,1024]{2,1,0:T(8,128)(2,1)} collective-permute-done((bf16[8,64,1024]{2,1,0:T(8,128)(2,1)}, bf16[8,64,1024]{2,1,0:T(8,128)(2,1)}, u32[]{:S(2)}, u32[]{:S(2)}) %collective-permute-start) | collective-permute-done | bytes 1048608 | tf_op jit(solution)/shard_map/cond/branch_1_fun/ppermute | solution.py:255
  59.7 1.2 %collective-permute-done.1 = bf16[8,64,1024]{2,1,0:T(8,128)(2,1)} collective-permute-done((bf16[8,64,1024]{2,1,0:T(8,128)(2,1)}, bf16[8,64,1024]{2,1,0:T(8,128)(2,1)}, u32[]{:S(2)}, u32[]{:S(2)}) %collective-permute-start.1) | collective-permute-done | bytes 1048608 | tf_op jit(solution)/shard_map/cond/branch_1_fun/ppermute | solution.py:255
  60.9 9.1 %all-to-all-done.1 = bf16[4,1056,128]{2,1,0:T(8,128)(2,1)} async-done(((bf16[4,1056,128]{2,1,0:T(8,128)(2,1)}), bf16[4,1056,128]{2,1,0:T(8,128)(2,1)}, u32[]{:S(2)}, u32[]{:S(2)}) %all-to-all-start.1) | async-done | bytes 1081376 | tf_op jit(solution)/shard_map/cond/branch_1_fun/all_to_all | solution.py:279
  69.9 0.0 copy-done.1
  69.9 1.9 %collective-permute-start.2 = (bf16[4,1056,128]{2,1,0:T(8,128)(2,1)}, bf16[4,1056,128]{2,1,0:T(8,128)(2,1)S(1)}, u32[]{:S(2)}, u32[]{:S(2)}) collective-permute-start(bf16[4,1056,128]{2,1,0:T(8,128)(2,1)} %get-tuple-element.26.s_ref.mine_ref), channel_id=1, source_target_pairs={{0,2},{2,0},{1,3},{3,1},{4,6},{6,4},{5,7},{7,5},{8,10},{10,8},{9,1... | collective-permute-start | bytes 3244040 | tf_op jit(solution)/shard_map/ppermute | solution.py:298
  71.9 0.0 collective-permute-done.3.g2
  71.9 0.0 copy-start
  71.9 3.1 %first_kernel.1 = f32[256,128]{1,0:T(8,128)S(1)} custom-call(bf16[4,1056,128]{2,1,0:T(8,128)(2,1)} %get-tuple-element.26.s_ref.mine_ref, bf16[8,64,1024]{2,1,0:T(8,128)(2,1)S(1)} %get-tuple-element.27.g0, bf16[8,64,1024]{2,1,0:T(8,128)(2,1)} %get-tuple-element.28.g1, bf16[8,64,1024]{2,1,0:T(8,128)(2,1)S(1)} %collective-permute-done.3.g2, ...), custom_call_target="tpu_custom_call" | custom-call | flops 32212254720 | bytes 3145728 | tf_op jit(solution)/shard_map/first_kernel/pallas_call | solution.py:215
  75.0 0.0 collective-permute-done.2.s_ref.other_ref
  75.0 0.0 copy-done
  75.0 3.1 %second_kernel.1 = f32[4,160,128]{2,1,0:T(8,128)S(1)} custom-call(bf16[4,1056,128]{2,1,0:T(8,128)(2,1)S(1)} %collective-permute-done.2.s_ref.other_ref, bf16[8,64,1024]{2,1,0:T(8,128)(2,1)S(1)} %get-tuple-element.27.g0, bf16[8,64,1024]{2,1,0:T(8,128)(2,1)} %get-tuple-element.28.g1, bf16[8,64,1024]{2,1,0:T(8,128)(2,1)S(1)} %collective-permute-done.3.g2, ...), custom_call_target="tpu_custom_call" | custom-call | flops 268435456 | bytes 3145728 | tf_op jit(solution)/shard_map/second_kernel/pallas_call | solution.py:215
  78.1 10.5 %all_to_all.13.in_ref = f32[4,160,128]{2,1,0:T(8,128)S(1)} all-to-all(f32[4,160,128]{2,1,0:T(8,128)S(1)} %second_kernel.1), channel_id=1, replica_groups=mesh['z'=16,'x'=4,'yl'=2,'core'=2,'yh'=2] {'yl','yh'}, dimensions={0} | all-to-all | bytes 655360 | tf_op jit(solution)/shard_map/all_to_all | solution.py:316
  88.6 1.0 %last.1 = (f32[2,2,32,64]{3,2,1,0:T(8,128)}, f32[2,2,32,64]{3,2,1,0:T(8,128)}) custom-call(f32[4,160,128]{2,1,0:T(8,128)S(1)} %all_to_all.13.in_ref), custom_call_target="tpu_custom_call" | custom-call | tf_op jit(solution)/shard_map/last/pallas_call | solution.py:318
Async XLA Ops:
  0.6 8.7 %copy-start.2 = (s32[2]{0:T(128)S(1)}, s32[2]{0:T(128)}, u32[]{:S(2)}) copy-start(s32[2]{0:T(128)} %fronts.1) | copy-start | bytes 28
  4.3 67.6 %collective-permute-start.3 = (bf16[8,64,1024]{2,1,0:T(8,128)(2,1)}, bf16[8,64,1024]{2,1,0:T(8,128)(2,1)S(1)}, u32[]{:S(2)}, u32[]{:S(2)}) collective-permute-start(bf16[8,64,1024]{2,1,0:T(8,128)(2,1)} %get-tuple-element.29), channel_id=1, source_target_pairs={{0,1},{4,5},{1,0},{5,4},{2,3},{6,7},{3,2},{7,6},{8,9},{12,13},{9,8... | collective-permute-start | bytes 3145736 | tf_op jit(solution)/shard_map/ppermute | solution.py:255
  12.1 37.5 %all-to-all-start = ((bf16[16,96,128]{2,1,0:T(8,128)(2,1)}), bf16[16,96,128]{2,1,0:T(8,128)(2,1)S(1)}, u32[]{:S(2)}, u32[]{:S(2)}) async-start(bf16[16,96,128]{2,1,0:T(8,128)(2,1)} %along_z.1), calls=%async_computation | async-start | bytes 786432 | tf_op jit(solution)/shard_map/cond/branch_1_fun/all_to_all | solution.py:270
  31.6 28.1 %collective-permute-start = (bf16[8,64,1024]{2,1,0:T(8,128)(2,1)}, bf16[8,64,1024]{2,1,0:T(8,128)(2,1)}, u32[]{:S(2)}, u32[]{:S(2)}) collective-permute-start(bf16[8,64,1024]{2,1,0:T(8,128)(2,1)} %get-tuple-element.13), channel_id=1, source_target_pairs={{0,4},{4,1},{1,5},{5,0},{2,6},{6,3},{3,7},{7,2},{8,12},{12,9},{9,1... | collective-permute-start | bytes 3145736 | tf_op jit(solution)/shard_map/cond/branch_1_fun/ppermute | solution.py:255
  34.2 26.7 %collective-permute-start.1 = (bf16[8,64,1024]{2,1,0:T(8,128)(2,1)}, bf16[8,64,1024]{2,1,0:T(8,128)(2,1)}, u32[]{:S(2)}, u32[]{:S(2)}) collective-permute-start(bf16[8,64,1024]{2,1,0:T(8,128)(2,1)} %get-tuple-element.14), channel_id=1, source_target_pairs={{0,5},{4,0},{1,4},{5,1},{2,7},{6,2},{3,6},{7,3},{8,13},{12,8},{9,1... | collective-permute-start | bytes 3145736 | tf_op jit(solution)/shard_map/cond/branch_1_fun/ppermute | solution.py:255
  50.7 19.3 %copy-start.1 = (bf16[8,64,1024]{2,1,0:T(8,128)(2,1)S(1)}, bf16[8,64,1024]{2,1,0:T(8,128)(2,1)}, u32[]{:S(2)}) copy-start(bf16[8,64,1024]{2,1,0:T(8,128)(2,1)} %get-tuple-element.36) | copy-start | bytes 3145732 | tf_op jit(solution)/shard_map/cond
  50.7 19.3 %all-to-all-start.1 = ((bf16[4,1056,128]{2,1,0:T(8,128)(2,1)}), bf16[4,1056,128]{2,1,0:T(8,128)(2,1)}, u32[]{:S(2)}, u32[]{:S(2)}) async-start(bf16[4,1056,128]{2,1,0:T(8,128)(2,1)} %along_x.1), calls=%async_computation.1 | async-start | bytes 2162688 | tf_op jit(solution)/shard_map/cond/branch_1_fun/all_to_all | solution.py:279
  69.9 5.0 %collective-permute-start.2 = (bf16[4,1056,128]{2,1,0:T(8,128)(2,1)}, bf16[4,1056,128]{2,1,0:T(8,128)(2,1)S(1)}, u32[]{:S(2)}, u32[]{:S(2)}) collective-permute-start(bf16[4,1056,128]{2,1,0:T(8,128)(2,1)} %get-tuple-element.26.s_ref.mine_ref), channel_id=1, source_target_pairs={{0,2},{2,0},{1,3},{3,1},{4,6},{6,4},{5,7},{7,5},{8,10},{10,8},{9,1... | collective-permute-start | bytes 3244040 | tf_op jit(solution)/shard_map/ppermute | solution.py:298
  71.9 3.1 %copy-start = (f32[2,2,32,64]{3,2,1,0:T(8,128)S(1)}, f32[2,2,32,64]{3,2,1,0:T(8,128)}, u32[]{:S(2)}) copy-start(f32[2,2,32,64]{3,2,1,0:T(8,128)} %prev_ref.1) | copy-start | bytes 98308

commit v5 on v4

--- a/solution.py
+++ b/solution.py
@@ -163,9 +163,16 @@
         out_ref[x, 1024:] = share
 
 
+def both_dots(s_ref, *pieces):
+    part = jnp.zeros((256, 128), F32)
+    for x in range(2):
+        rows = jnp.concatenate([piece[x] for piece in pieces], axis=0)
+        part = part + jnp.dot(rows, s_ref[x, :1024], preferred_element_type=F32)
+    return part
+
+
 def first_kernel(s_ref, g0, g1, g2, g3, out_ref):
-    rows = jnp.concatenate([g0[0], g1[0], g2[0], g3[0]], axis=0)
-    part = jnp.dot(rows, s_ref[0, :1024], preferred_element_type=F32)
+    part = both_dots(s_ref, g0, g1, g2, g3)
 
     @pl.when(pl.program_id(0) == 0)
     def _():
@@ -177,8 +184,7 @@
 
 
 def second_kernel(s_ref, g0, g1, g2, g3, part_ref, mine_ref, other_ref, prev_ref, out_ref, total):
-    rows = jnp.concatenate([g0[0], g1[0], g2[0], g3[0]], axis=0)
-    part = jnp.dot(rows, s_ref[0, :1024], preferred_element_type=F32).reshape(4, 64, 128)
+    part = both_dots(s_ref, g0, g1, g2, g3).reshape(4, 64, 128)
     step = pl.program_id(0)
 
     @pl.when(step == 0)
@@ -189,7 +195,7 @@
     def _():
         total[...] += part
 
-    @pl.when(step == 3)
+    @pl.when(step == 1)
     def _():
         core, yl, yh = lax.axis_index("core"), lax.axis_index("yl"), lax.axis_index("yh")
         before = [prev_ref[f].reshape(64, 64) for f in range(2)]
@@ -214,9 +220,9 @@
 def dots(s, pieces, half, extra=(), extra_specs=(), kernel=first_kernel, out=(256, 128), scratch=()):
     return pl.pallas_call(
         kernel,
-        grid=(4,),
-        in_specs=[pl.BlockSpec((1, 1056, 128), lambda i: (i, 0, 0))]
-        + [pl.BlockSpec((1, 64, 1024), lambda i: (half * 4 + i, 0, 0))] * 4
+        grid=(2,),
+        in_specs=[pl.BlockSpec((2, 1056, 128), lambda i: (i, 0, 0))]
+        + [pl.BlockSpec((2, 64, 1024), lambda i: (half * 2 + i, 0, 0))] * 4
         + list(extra_specs),
         out_specs=pl.BlockSpec(out, lambda i: (0,) * len(out)),
         out_shape=VMEM(out, F32),

time: 90.2 us -> 88.5 us (0.981)
  Pallas kernels: 17.1 us -> 15.1 us
    pallas_call x2, Pallas kernels: 6.17 us -> 4.2 us  [dots(): pl.pallas_call(kernel, grid=(2,), in_specs=[pl.BlockSpec((2, 1056, 128),...]
  transfers between devices with their start and end apart: 6 -> 6, of which waited for: 4 -> 5; matrix products, arithmetic and copies ran while one was open for 0% -> 0% of each run, Pallas kernels for 10% -> 10%
where the time goes in v5:
time: 88.5 us; the launch traced here: 88 us
  starting transfers between devices  33.7 us (38%)
  waiting for transfers between devices  26.4 us (30%)
  Pallas kernels  15.1 us (17%)
  blocking collectives  12 us (14%)
    all_to_all x1, starting transfers between devices, gathered(): message = lax.all_to_all(message, 'z', 0, 0, tiled=True)  15.2 us
    ppermute x3, starting transfers between devices, along_ring(): lax.ppermute(piece, RING, [(ring_index(y), ring_index((y + d) % 4)) for y...  12.1 us
    all_to_all x1, waiting for transfers between devices, gathered(): message = lax.all_to_all(message, 'z', 0, 0, tiled=True)  10.9 us
    all_to_all x1, blocking collectives, body(): sums = lax.all_to_all(sums, RING, 0, 0, tiled=True)  10.1 us
    all_to_all x1, waiting for transfers between devices, gathered(): return (lax.all_to_all(message, 'x', 0, 0, tiled=True), own, first, third)  9.06 us
    ppermute x3, waiting for transfers between devices, along_ring(): lax.ppermute(piece, RING, [(ring_index(y), ring_index((y + d) % 4)) for y...  5.79 us
    all_to_all x1, starting transfers between devices, gathered(): return (lax.all_to_all(message, 'x', 0, 0, tiled=True), own, first, third)  4.42 us
    pallas_call x1, Pallas kernels, prep_others(): pl.pallas_call(others_kernel, grid=(8 // PAIRS,), in_specs=[whole(SMEM),...  4.34 us
  transfers between devices with their start and end apart: 6, of which 5 were waited for; matrix products, arithmetic and copies ran while one was open for 0% of the time, Pallas kernels for 10%

profile of v5, /device:TPU:32, one launch (start us, length us, event | category | flops | bytes accessed | tf_op | source)
XLA Modules:
  0.0 88.0 jit_solution(4871329153076241633)
XLA Ops:
  0.6 0.0 copy-start.2
  0.6 3.6 %prep_opposite.1 = (bf16[8,64,1024]{2,1,0:T(8,128)(2,1)}, f32[32,128]{1,0:T(8,128)S(1)}, bf16[64,128]{1,0:T(8,128)(2,1)S(1)}) custom-call(s32[256]{0:T(256)} %slots.1, s32[2]{0:T(128)} %fronts.1, bf16[64,32768]{1,0:T(8,128)(2,1)} %bitcast.8, bf16[128,128]{1,0:T(8,128)(2,1)} %bitcast.10, f32[2,64,64]{2,1,0:T(8,128)} %inv_ref.1), custom_call_target="tpu_custom_call" | custom-call | tf_op jit(solution)/shard_map/prep_opposite/pallas_call | solution.py:113
  4.3 5.1 %collective-permute-start.3 = (bf16[8,64,1024]{2,1,0:T(8,128)(2,1)}, bf16[8,64,1024]{2,1,0:T(8,128)(2,1)S(1)}, u32[]{:S(2)}, u32[]{:S(2)}) collective-permute-start(bf16[8,64,1024]{2,1,0:T(8,128)(2,1)} %get-tuple-element.29), channel_id=1, source_target_pairs={{0,1},{4,5},{1,0},{5,4},{2,3},{6,7},{3,2},{7,6},{8,9},{12,13},{9,8... | collective-permute-start | bytes 3145736 | tf_op jit(solution)/shard_map/ppermute | solution.py:261
  9.4 0.0 copy-done.2
  9.4 60.5 %conditional.1 = (bf16[4,1056,128]{2,1,0:T(8,128)(2,1)}, bf16[8,64,1024]{2,1,0:T(8,128)(2,1)S(1)}, bf16[8,64,1024]{2,1,0:T(8,128)(2,1)}, bf16[8,64,1024]{2,1,0:T(8,128)(2,1)}) conditional(s32[]{:T(128)} %bitcast.1, () %tuple.15, (f32[32,128]{1,0:T(8,128)S(1)}, bf16[64,128]{1,0:T(8,128)(2,1)S(1)}, s32[256]{0:T(256)}, bf16[64,32768]{1,0:T(8,128)(2,1)}) %tuple.19), branch_computations={%region_0.0_spmd, %region_1.0_spmd} | conditional | flops 536870912 | bytes 23347404 | solution.py:294
  9.4 1.8 %all-gather = f32[64,128]{1,0:T(8,128)S(1)} all-gather(f32[32,128]{1,0:T(8,128)S(1)} %get-tuple-element.8), channel_id=2, replica_groups=mesh['z'=16,'x'=4,'yl'=2,'core'=2,'yh'=2] {'core'}, dimensions={0}, use_global_device_ids=true | all-gather | bytes 49152 | tf_op jit(solution)/shard_map/cond/branch_1_fun/all_gather | solution.py:267
  11.3 0.8 along_z.1
  12.1 15.2 %all-to-all-start = ((bf16[16,96,128]{2,1,0:T(8,128)(2,1)}), bf16[16,96,128]{2,1,0:T(8,128)(2,1)S(1)}, u32[]{:S(2)}, u32[]{:S(2)}) async-start(bf16[16,96,128]{2,1,0:T(8,128)(2,1)} %along_z.1), calls=%async_computation | async-start | bytes 786432 | tf_op jit(solution)/shard_map/cond/branch_1_fun/all_to_all | solution.py:276
  27.3 4.3 %prep_others.1 = (bf16[8,64,1024]{2,1,0:T(8,128)(2,1)}, bf16[8,64,1024]{2,1,0:T(8,128)(2,1)}, bf16[8,64,1024]{2,1,0:T(8,128)(2,1)}) custom-call(s32[256]{0:T(256)} %get-tuple-element.10.slots, bf16[64,32768]{1,0:T(8,128)(2,1)} %get-tuple-element.11.g_ref), custom_call_target="tpu_custom_call" | custom-call | flops 536870912 | bytes 6291456 | tf_op jit(solution)/shard_map/cond/branch_1_fun/prep_others/pallas_call | solution.py:132
  31.6 2.6 %collective-permute-start = (bf16[8,64,1024]{2,1,0:T(8,128)(2,1)}, bf16[8,64,1024]{2,1,0:T(8,128)(2,1)}, u32[]{:S(2)}, u32[]{:S(2)}) collective-permute-start(bf16[8,64,1024]{2,1,0:T(8,128)(2,1)} %get-tuple-element.13), channel_id=1, source_target_pairs={{0,4},{4,1},{1,5},{5,0},{2,6},{6,3},{3,7},{7,2},{8,12},{12,9},{9,1... | collective-permute-start | bytes 3145736 | tf_op jit(solution)/shard_map/cond/branch_1_fun/ppermute | solution.py:261
  34.2 4.5 %collective-permute-start.1 = (bf16[8,64,1024]{2,1,0:T(8,128)(2,1)}, bf16[8,64,1024]{2,1,0:T(8,128)(2,1)}, u32[]{:S(2)}, u32[]{:S(2)}) collective-permute-start(bf16[8,64,1024]{2,1,0:T(8,128)(2,1)} %get-tuple-element.14), channel_id=1, source_target_pairs={{0,5},{4,0},{1,4},{5,1},{2,7},{6,2},{3,6},{7,3},{8,13},{12,8},{9,1... | collective-permute-start | bytes 3145736 | tf_op jit(solution)/shard_map/cond/branch_1_fun/ppermute | solution.py:261
  38.7 10.9 %all-to-all-done.in_ref = bf16[16,96,128]{2,1,0:T(8,128)(2,1)S(1)} async-done(((bf16[16,96,128]{2,1,0:T(8,128)(2,1)}), bf16[16,96,128]{2,1,0:T(8,128)(2,1)S(1)}, u32[]{:S(2)}, u32[]{:S(2)}) %all-to-all-start) | async-done | bytes 393248 | tf_op jit(solution)/shard_map/cond/branch_1_fun/all_to_all | solution.py:276
  49.5 1.1 %along_x.1 = bf16[4,1056,128]{2,1,0:T(8,128)(2,1)} custom-call(bf16[16,96,128]{2,1,0:T(8,128)(2,1)S(1)} %all-to-all-done.in_ref), custom_call_target="tpu_custom_call" | custom-call | tf_op jit(solution)/shard_map/cond/branch_1_fun/along_x/pallas_call | solution.py:277
  50.7 0.0 copy-start.1
  50.7 4.4 %all-to-all-start.1 = ((bf16[4,1056,128]{2,1,0:T(8,128)(2,1)}), bf16[4,1056,128]{2,1,0:T(8,128)(2,1)}, u32[]{:S(2)}, u32[]{:S(2)}) async-start(bf16[4,1056,128]{2,1,0:T(8,128)(2,1)} %along_x.1), calls=%async_computation.1 | async-start | bytes 2162688 | tf_op jit(solution)/shard_map/cond/branch_1_fun/all_to_all | solution.py:285
  55.1 4.6 %collective-permute-done = bf16[8,64,1024]{2,1,0:T(8,128)(2,1)} collective-permute-done((bf16[8,64,1024]{2,1,0:T(8,128)(2,1)}, bf16[8,64,1024]{2,1,0:T(8,128)(2,1)}, u32[]{:S(2)}, u32[]{:S(2)}) %collective-permute-start) | collective-permute-done | bytes 1048608 | tf_op jit(solution)/shard_map/cond/branch_1_fun/ppermute | solution.py:261
  59.7 1.2 %collective-permute-done.1 = bf16[8,64,1024]{2,1,0:T(8,128)(2,1)} collective-permute-done((bf16[8,64,1024]{2,1,0:T(8,128)(2,1)}, bf16[8,64,1024]{2,1,0:T(8,128)(2,1)}, u32[]{:S(2)}, u32[]{:S(2)}) %collective-permute-start.1) | collective-permute-done | bytes 1048608 | tf_op jit(solution)/shard_map/cond/branch_1_fun/ppermute | solution.py:261
  60.9 9.1 %all-to-all-done.1 = bf16[4,1056,128]{2,1,0:T(8,128)(2,1)} async-done(((bf16[4,1056,128]{2,1,0:T(8,128)(2,1)}), bf16[4,1056,128]{2,1,0:T(8,128)(2,1)}, u32[]{:S(2)}, u32[]{:S(2)}) %all-to-all-start.1) | async-done | bytes 1081376 | tf_op jit(solution)/shard_map/cond/branch_1_fun/all_to_all | solution.py:285
  69.9 0.0 copy-done.1
  69.9 1.9 %collective-permute-start.2 = (bf16[4,1056,128]{2,1,0:T(8,128)(2,1)}, bf16[4,1056,128]{2,1,0:T(8,128)(2,1)S(1)}, u32[]{:S(2)}, u32[]{:S(2)}) collective-permute-start(bf16[4,1056,128]{2,1,0:T(8,128)(2,1)} %get-tuple-element.26.s_ref.mine_ref), channel_id=1, source_target_pairs={{0,2},{2,0},{1,3},{3,1},{4,6},{6,4},{5,7},{7,5},{8,10},{10,8},{9,1... | collective-permute-start | bytes 3244040 | tf_op jit(solution)/shard_map/ppermute | solution.py:304
  71.9 0.0 collective-permute-done.3.g2
  71.9 0.0 copy-start
  71.9 2.1 %first_kernel.1 = f32[256,128]{1,0:T(8,128)S(1)} custom-call(bf16[4,1056,128]{2,1,0:T(8,128)(2,1)} %get-tuple-element.26.s_ref.mine_ref, bf16[8,64,1024]{2,1,0:T(8,128)(2,1)S(1)} %get-tuple-element.27.g0, bf16[8,64,1024]{2,1,0:T(8,128)(2,1)} %get-tuple-element.28.g1, bf16[8,64,1024]{2,1,0:T(8,128)(2,1)S(1)} %collective-permute-done.3.g2, ...), custom_call_target="tpu_custom_call" | custom-call | flops 32212254720 | bytes 3145728 | tf_op jit(solution)/shard_map/first_kernel/pallas_call | solution.py:221
  74.0 0.7 collective-permute-done.2.s_ref.other_ref
  74.7 0.0 copy-done
  74.8 2.1 %second_kernel.1 = f32[4,160,128]{2,1,0:T(8,128)S(1)} custom-call(bf16[4,1056,128]{2,1,0:T(8,128)(2,1)S(1)} %collective-permute-done.2.s_ref.other_ref, bf16[8,64,1024]{2,1,0:T(8,128)(2,1)S(1)} %get-tuple-element.27.g0, bf16[8,64,1024]{2,1,0:T(8,128)(2,1)} %get-tuple-element.28.g1, bf16[8,64,1024]{2,1,0:T(8,128)(2,1)S(1)} %collective-permute-done.3.g2, ...), custom_call_target="tpu_custom_call" | custom-call | flops 268435456 | bytes 3145728 | tf_op jit(solution)/shard_map/second_kernel/pallas_call | solution.py:221
  76.8 10.1 %all_to_all.13.in_ref = f32[4,160,128]{2,1,0:T(8,128)S(1)} all-to-all(f32[4,160,128]{2,1,0:T(8,128)S(1)} %second_kernel.1), channel_id=1, replica_groups=mesh['z'=16,'x'=4,'yl'=2,'core'=2,'yh'=2] {'yl','yh'}, dimensions={0} | all-to-all | bytes 655360 | tf_op jit(solution)/shard_map/all_to_all | solution.py:322
  87.0 1.0 %last.1 = (f32[2,2,32,64]{3,2,1,0:T(8,128)}, f32[2,2,32,64]{3,2,1,0:T(8,128)}) custom-call(f32[4,160,128]{2,1,0:T(8,128)S(1)} %all_to_all.13.in_ref), custom_call_target="tpu_custom_call" | custom-call | tf_op jit(solution)/shard_map/last/pallas_call | solution.py:324
Async XLA Ops:
  0.6 8.7 %copy-start.2 = (s32[2]{0:T(128)S(1)}, s32[2]{0:T(128)}, u32[]{:S(2)}) copy-start(s32[2]{0:T(128)} %fronts.1) | copy-start | bytes 28
  4.3 67.6 %collective-permute-start.3 = (bf16[8,64,1024]{2,1,0:T(8,128)(2,1)}, bf16[8,64,1024]{2,1,0:T(8,128)(2,1)S(1)}, u32[]{:S(2)}, u32[]{:S(2)}) collective-permute-start(bf16[8,64,1024]{2,1,0:T(8,128)(2,1)} %get-tuple-element.29), channel_id=1, source_target_pairs={{0,1},{4,5},{1,0},{5,4},{2,3},{6,7},{3,2},{7,6},{8,9},{12,13},{9,8... | collective-permute-start | bytes 3145736 | tf_op jit(solution)/shard_map/ppermute | solution.py:261
  12.1 37.5 %all-to-all-start = ((bf16[16,96,128]{2,1,0:T(8,128)(2,1)}), bf16[16,96,128]{2,1,0:T(8,128)(2,1)S(1)}, u32[]{:S(2)}, u32[]{:S(2)}) async-start(bf16[16,96,128]{2,1,0:T(8,128)(2,1)} %along_z.1), calls=%async_computation | async-start | bytes 786432 | tf_op jit(solution)/shard_map/cond/branch_1_fun/all_to_all | solution.py:276
  31.6 28.1 %collective-permute-start = (bf16[8,64,1024]{2,1,0:T(8,128)(2,1)}, bf16[8,64,1024]{2,1,0:T(8,128)(2,1)}, u32[]{:S(2)}, u32[]{:S(2)}) collective-permute-start(bf16[8,64,1024]{2,1,0:T(8,128)(2,1)} %get-tuple-element.13), channel_id=1, source_target_pairs={{0,4},{4,1},{1,5},{5,0},{2,6},{6,3},{3,7},{7,2},{8,12},{12,9},{9,1... | collective-permute-start | bytes 3145736 | tf_op jit(solution)/shard_map/cond/branch_1_fun/ppermute | solution.py:261
  34.2 26.7 %collective-permute-start.1 = (bf16[8,64,1024]{2,1,0:T(8,128)(2,1)}, bf16[8,64,1024]{2,1,0:T(8,128)(2,1)}, u32[]{:S(2)}, u32[]{:S(2)}) collective-permute-start(bf16[8,64,1024]{2,1,0:T(8,128)(2,1)} %get-tuple-element.14), channel_id=1, source_target_pairs={{0,5},{4,0},{1,4},{5,1},{2,7},{6,2},{3,6},{7,3},{8,13},{12,8},{9,1... | collective-permute-start | bytes 3145736 | tf_op jit(solution)/shard_map/cond/branch_1_fun/ppermute | solution.py:261
  50.7 19.3 %copy-start.1 = (bf16[8,64,1024]{2,1,0:T(8,128)(2,1)S(1)}, bf16[8,64,1024]{2,1,0:T(8,128)(2,1)}, u32[]{:S(2)}) copy-start(bf16[8,64,1024]{2,1,0:T(8,128)(2,1)} %get-tuple-element.36) | copy-start | bytes 3145732 | tf_op jit(solution)/shard_map/cond
  50.7 19.3 %all-to-all-start.1 = ((bf16[4,1056,128]{2,1,0:T(8,128)(2,1)}), bf16[4,1056,128]{2,1,0:T(8,128)(2,1)}, u32[]{:S(2)}, u32[]{:S(2)}) async-start(bf16[4,1056,128]{2,1,0:T(8,128)(2,1)} %along_x.1), calls=%async_computation.1 | async-start | bytes 2162688 | tf_op jit(solution)/shard_map/cond/branch_1_fun/all_to_all | solution.py:285
  69.9 4.8 %collective-permute-start.2 = (bf16[4,1056,128]{2,1,0:T(8,128)(2,1)}, bf16[4,1056,128]{2,1,0:T(8,128)(2,1)S(1)}, u32[]{:S(2)}, u32[]{:S(2)}) collective-permute-start(bf16[4,1056,128]{2,1,0:T(8,128)(2,1)} %get-tuple-element.26.s_ref.mine_ref), channel_id=1, source_target_pairs={{0,2},{2,0},{1,3},{3,1},{4,6},{6,4},{5,7},{7,5},{8,10},{10,8},{9,1... | collective-permute-start | bytes 3244040 | tf_op jit(solution)/shard_map/ppermute | solution.py:304
  71.9 2.9 %copy-start = (f32[2,2,32,64]{3,2,1,0:T(8,128)S(1)}, f32[2,2,32,64]{3,2,1,0:T(8,128)}, u32[]{:S(2)}) copy-start(f32[2,2,32,64]{3,2,1,0:T(8,128)} %prev_ref.1) | copy-start | bytes 98308

commit v6 on v5

--- a/solution.py
+++ b/solution.py
@@ -165,7 +165,7 @@
 
 def both_dots(s_ref, *pieces):
     part = jnp.zeros((256, 128), F32)
-    for x in range(2):
+    for x in range(4):
         rows = jnp.concatenate([piece[x] for piece in pieces], axis=0)
         part = part + jnp.dot(rows, s_ref[x, :1024], preferred_element_type=F32)
     return part
@@ -195,7 +195,7 @@
     def _():
         total[...] += part
 
-    @pl.when(step == 1)
+    @pl.when(step == 0)
     def _():
         core, yl, yh = lax.axis_index("core"), lax.axis_index("yl"), lax.axis_index("yh")
         before = [prev_ref[f].reshape(64, 64) for f in range(2)]
@@ -220,9 +220,9 @@
 def dots(s, pieces, half, extra=(), extra_specs=(), kernel=first_kernel, out=(256, 128), scratch=()):
     return pl.pallas_call(
         kernel,
-        grid=(2,),
-        in_specs=[pl.BlockSpec((2, 1056, 128), lambda i: (i, 0, 0))]
-        + [pl.BlockSpec((2, 64, 1024), lambda i: (half * 2 + i, 0, 0))] * 4
+        grid=(1,),
+        in_specs=[pl.BlockSpec((4, 1056, 128), lambda i: (i, 0, 0))]
+        + [pl.BlockSpec((4, 64, 1024), lambda i: (half + i, 0, 0))] * 4
         + list(extra_specs),
         out_specs=pl.BlockSpec(out, lambda i: (0,) * len(out)),
         out_shape=VMEM(out, F32),

time: 88.5 us -> 88.3 us (level)
  no operation moved by 1% of the time
where the time goes in v6:
time: 88.3 us; the launch traced here: 87.9 us
  starting transfers between devices  33.7 us (38%)
  waiting for transfers between devices  26.3 us (30%)
  Pallas kernels  15.1 us (17%)
  blocking collectives  12 us (14%)
    all_to_all x1, starting transfers between devices, gathered(): message = lax.all_to_all(message, 'z', 0, 0, tiled=True)  15.2 us
    ppermute x3, starting transfers between devices, along_ring(): lax.ppermute(piece, RING, [(ring_index(y), ring_index((y + d) % 4)) for y...  12.1 us
    all_to_all x1, waiting for transfers between devices, gathered(): message = lax.all_to_all(message, 'z', 0, 0, tiled=True)  10.9 us
    all_to_all x1, blocking collectives, body(): sums = lax.all_to_all(sums, RING, 0, 0, tiled=True)  10.1 us
    all_to_all x1, waiting for transfers between devices, gathered(): return (lax.all_to_all(message, 'x', 0, 0, tiled=True), own, first, third)  9.06 us
    ppermute x3, waiting for transfers between devices, along_ring(): lax.ppermute(piece, RING, [(ring_index(y), ring_index((y + d) % 4)) for y...  5.79 us
    all_to_all x1, starting transfers between devices, gathered(): return (lax.all_to_all(message, 'x', 0, 0, tiled=True), own, first, third)  4.42 us
    pallas_call x1, Pallas kernels, prep_others(): pl.pallas_call(others_kernel, grid=(8 // PAIRS,), in_specs=[whole(SMEM),...  4.34 us
  transfers between devices with their start and end apart: 6, of which 5 were waited for; matrix products, arithmetic and copies ran while one was open for 0% of the time, Pallas kernels for 10%

profile of v6, /device:TPU:32, one launch (start us, length us, event | category | flops | bytes accessed | tf_op | source)
XLA Modules:
  0.0 87.9 jit_solution(15327030003570847087)
XLA Ops:
  0.6 0.0 copy-start.2
  0.6 3.6 %prep_opposite.1 = (bf16[8,64,1024]{2,1,0:T(8,128)(2,1)}, f32[32,128]{1,0:T(8,128)S(1)}, bf16[64,128]{1,0:T(8,128)(2,1)S(1)}) custom-call(s32[256]{0:T(256)} %slots.1, s32[2]{0:T(128)} %fronts.1, bf16[64,32768]{1,0:T(8,128)(2,1)} %bitcast.8, bf16[128,128]{1,0:T(8,128)(2,1)} %bitcast.10, f32[2,64,64]{2,1,0:T(8,128)} %inv_ref.1), custom_call_target="tpu_custom_call" | custom-call | tf_op jit(solution)/shard_map/prep_opposite/pallas_call | solution.py:113
  4.3 5.1 %collective-permute-start.3 = (bf16[8,64,1024]{2,1,0:T(8,128)(2,1)}, bf16[8,64,1024]{2,1,0:T(8,128)(2,1)S(1)}, u32[]{:S(2)}, u32[]{:S(2)}) collective-permute-start(bf16[8,64,1024]{2,1,0:T(8,128)(2,1)} %get-tuple-element.29), channel_id=1, source_target_pairs={{0,1},{4,5},{1,0},{5,4},{2,3},{6,7},{3,2},{7,6},{8,9},{12,13},{9,8... | collective-permute-start | bytes 3145736 | tf_op jit(solution)/shard_map/ppermute | solution.py:261
  9.4 0.0 copy-done.2
  9.4 60.5 %conditional.1 = (bf16[4,1056,128]{2,1,0:T(8,128)(2,1)}, bf16[8,64,1024]{2,1,0:T(8,128)(2,1)S(1)}, bf16[8,64,1024]{2,1,0:T(8,128)(2,1)}, bf16[8,64,1024]{2,1,0:T(8,128)(2,1)}) conditional(s32[]{:T(128)} %bitcast.1, () %tuple.15, (f32[32,128]{1,0:T(8,128)S(1)}, bf16[64,128]{1,0:T(8,128)(2,1)S(1)}, s32[256]{0:T(256)}, bf16[64,32768]{1,0:T(8,128)(2,1)}) %tuple.19), branch_computations={%region_0.0_spmd, %region_1.0_spmd} | conditional | flops 536870912 | bytes 23347404 | solution.py:294
  9.4 1.8 %all-gather = f32[64,128]{1,0:T(8,128)S(1)} all-gather(f32[32,128]{1,0:T(8,128)S(1)} %get-tuple-element.8), channel_id=2, replica_groups=mesh['z'=16,'x'=4,'yl'=2,'core'=2,'yh'=2] {'core'}, dimensions={0}, use_global_device_ids=true | all-gather | bytes 49152 | tf_op jit(solution)/shard_map/cond/branch_1_fun/all_gather | solution.py:267
  11.3 0.8 along_z.1
  12.1 15.2 %all-to-all-start = ((bf16[16,96,128]{2,1,0:T(8,128)(2,1)}), bf16[16,96,128]{2,1,0:T(8,128)(2,1)S(1)}, u32[]{:S(2)}, u32[]{:S(2)}) async-start(bf16[16,96,128]{2,1,0:T(8,128)(2,1)} %along_z.1), calls=%async_computation | async-start | bytes 786432 | tf_op jit(solution)/shard_map/cond/branch_1_fun/all_to_all | solution.py:276
  27.3 4.3 %prep_others.1 = (bf16[8,64,1024]{2,1,0:T(8,128)(2,1)}, bf16[8,64,1024]{2,1,0:T(8,128)(2,1)}, bf16[8,64,1024]{2,1,0:T(8,128)(2,1)}) custom-call(s32[256]{0:T(256)} %get-tuple-element.10.slots, bf16[64,32768]{1,0:T(8,128)(2,1)} %get-tuple-element.11.g_ref), custom_call_target="tpu_custom_call" | custom-call | flops 536870912 | bytes 6291456 | tf_op jit(solution)/shard_map/cond/branch_1_fun/prep_others/pallas_call | solution.py:132
  31.6 2.6 %collective-permute-start = (bf16[8,64,1024]{2,1,0:T(8,128)(2,1)}, bf16[8,64,1024]{2,1,0:T(8,128)(2,1)}, u32[]{:S(2)}, u32[]{:S(2)}) collective-permute-start(bf16[8,64,1024]{2,1,0:T(8,128)(2,1)} %get-tuple-element.13), channel_id=1, source_target_pairs={{0,4},{4,1},{1,5},{5,0},{2,6},{6,3},{3,7},{7,2},{8,12},{12,9},{9,1... | collective-permute-start | bytes 3145736 | tf_op jit(solution)/shard_map/cond/branch_1_fun/ppermute | solution.py:261
  34.2 4.5 %collective-permute-start.1 = (bf16[8,64,1024]{2,1,0:T(8,128)(2,1)}, bf16[8,64,1024]{2,1,0:T(8,128)(2,1)}, u32[]{:S(2)}, u32[]{:S(2)}) collective-permute-start(bf16[8,64,1024]{2,1,0:T(8,128)(2,1)} %get-tuple-element.14), channel_id=1, source_target_pairs={{0,5},{4,0},{1,4},{5,1},{2,7},{6,2},{3,6},{7,3},{8,13},{12,8},{9,1... | collective-permute-start | bytes 3145736 | tf_op jit(solution)/shard_map/cond/branch_1_fun/ppermute | solution.py:261
  38.7 10.9 %all-to-all-done.in_ref = bf16[16,96,128]{2,1,0:T(8,128)(2,1)S(1)} async-done(((bf16[16,96,128]{2,1,0:T(8,128)(2,1)}), bf16[16,96,128]{2,1,0:T(8,128)(2,1)S(1)}, u32[]{:S(2)}, u32[]{:S(2)}) %all-to-all-start) | async-done | bytes 393248 | tf_op jit(solution)/shard_map/cond/branch_1_fun/all_to_all | solution.py:276
  49.5 1.1 %along_x.1 = bf16[4,1056,128]{2,1,0:T(8,128)(2,1)} custom-call(bf16[16,96,128]{2,1,0:T(8,128)(2,1)S(1)} %all-to-all-done.in_ref), custom_call_target="tpu_custom_call" | custom-call | tf_op jit(solution)/shard_map/cond/branch_1_fun/along_x/pallas_call | solution.py:277
  50.7 0.0 copy-start.1
  50.7 4.4 %all-to-all-start.1 = ((bf16[4,1056,128]{2,1,0:T(8,128)(2,1)}), bf16[4,1056,128]{2,1,0:T(8,128)(2,1)}, u32[]{:S(2)}, u32[]{:S(2)}) async-start(bf16[4,1056,128]{2,1,0:T(8,128)(2,1)} %along_x.1), calls=%async_computation.1 | async-start | bytes 2162688 | tf_op jit(solution)/shard_map/cond/branch_1_fun/all_to_all | solution.py:285
  55.1 4.6 %collective-permute-done = bf16[8,64,1024]{2,1,0:T(8,128)(2,1)} collective-permute-done((bf16[8,64,1024]{2,1,0:T(8,128)(2,1)}, bf16[8,64,1024]{2,1,0:T(8,128)(2,1)}, u32[]{:S(2)}, u32[]{:S(2)}) %collective-permute-start) | collective-permute-done | bytes 1048608 | tf_op jit(solution)/shard_map/cond/branch_1_fun/ppermute | solution.py:261
  59.7 1.2 %collective-permute-done.1 = bf16[8,64,1024]{2,1,0:T(8,128)(2,1)} collective-permute-done((bf16[8,64,1024]{2,1,0:T(8,128)(2,1)}, bf16[8,64,1024]{2,1,0:T(8,128)(2,1)}, u32[]{:S(2)}, u32[]{:S(2)}) %collective-permute-start.1) | collective-permute-done | bytes 1048608 | tf_op jit(solution)/shard_map/cond/branch_1_fun/ppermute | solution.py:261
  60.9 9.1 %all-to-all-done.1 = bf16[4,1056,128]{2,1,0:T(8,128)(2,1)} async-done(((bf16[4,1056,128]{2,1,0:T(8,128)(2,1)}), bf16[4,1056,128]{2,1,0:T(8,128)(2,1)}, u32[]{:S(2)}, u32[]{:S(2)}) %all-to-all-start.1) | async-done | bytes 1081376 | tf_op jit(solution)/shard_map/cond/branch_1_fun/all_to_all | solution.py:285
  69.9 0.0 copy-done.1
  69.9 1.9 %collective-permute-start.2 = (bf16[4,1056,128]{2,1,0:T(8,128)(2,1)}, bf16[4,1056,128]{2,1,0:T(8,128)(2,1)S(1)}, u32[]{:S(2)}, u32[]{:S(2)}) collective-permute-start(bf16[4,1056,128]{2,1,0:T(8,128)(2,1)} %get-tuple-element.26.s_ref.mine_ref), channel_id=1, source_target_pairs={{0,2},{2,0},{1,3},{3,1},{4,6},{6,4},{5,7},{7,5},{8,10},{10,8},{9,1... | collective-permute-start | bytes 3244040 | tf_op jit(solution)/shard_map/ppermute | solution.py:304
  71.9 0.0 collective-permute-done.3.g2
  71.9 0.0 copy-start
  71.9 2.2 %first_kernel.1 = f32[256,128]{1,0:T(8,128)S(1)} custom-call(bf16[4,1056,128]{2,1,0:T(8,128)(2,1)} %get-tuple-element.26.s_ref.mine_ref, bf16[8,64,1024]{2,1,0:T(8,128)(2,1)S(1)} %get-tuple-element.27.g0, bf16[8,64,1024]{2,1,0:T(8,128)(2,1)} %get-tuple-element.28.g1, bf16[8,64,1024]{2,1,0:T(8,128)(2,1)S(1)} %collective-permute-done.3.g2, ...), custom_call_target="tpu_custom_call" | custom-call | flops 32212254720 | bytes 3145728 | tf_op jit(solution)/shard_map/first_kernel/pallas_call | solution.py:221
  74.1 0.6 collective-permute-done.2.s_ref.other_ref
  74.7 0.0 copy-done
  74.8 1.9 %second_kernel.1 = f32[4,160,128]{2,1,0:T(8,128)S(1)} custom-call(bf16[4,1056,128]{2,1,0:T(8,128)(2,1)S(1)} %collective-permute-done.2.s_ref.other_ref, bf16[8,64,1024]{2,1,0:T(8,128)(2,1)S(1)} %get-tuple-element.27.g0, bf16[8,64,1024]{2,1,0:T(8,128)(2,1)} %get-tuple-element.28.g1, bf16[8,64,1024]{2,1,0:T(8,128)(2,1)S(1)} %collective-permute-done.3.g2, ...), custom_call_target="tpu_custom_call" | custom-call | flops 268435456 | bytes 3145728 | tf_op jit(solution)/shard_map/second_kernel/pallas_call | solution.py:221
  76.7 10.1 %all_to_all.13.in_ref = f32[4,160,128]{2,1,0:T(8,128)S(1)} all-to-all(f32[4,160,128]{2,1,0:T(8,128)S(1)} %second_kernel.1), channel_id=1, replica_groups=mesh['z'=16,'x'=4,'yl'=2,'core'=2,'yh'=2] {'yl','yh'}, dimensions={0} | all-to-all | bytes 655360 | tf_op jit(solution)/shard_map/all_to_all | solution.py:322
  86.8 1.0 %last.1 = (f32[2,2,32,64]{3,2,1,0:T(8,128)}, f32[2,2,32,64]{3,2,1,0:T(8,128)}) custom-call(f32[4,160,128]{2,1,0:T(8,128)S(1)} %all_to_all.13.in_ref), custom_call_target="tpu_custom_call" | custom-call | tf_op jit(solution)/shard_map/last/pallas_call | solution.py:324
Async XLA Ops:
  0.6 8.7 %copy-start.2 = (s32[2]{0:T(128)S(1)}, s32[2]{0:T(128)}, u32[]{:S(2)}) copy-start(s32[2]{0:T(128)} %fronts.1) | copy-start | bytes 28
  4.3 67.6 %collective-permute-start.3 = (bf16[8,64,1024]{2,1,0:T(8,128)(2,1)}, bf16[8,64,1024]{2,1,0:T(8,128)(2,1)S(1)}, u32[]{:S(2)}, u32[]{:S(2)}) collective-permute-start(bf16[8,64,1024]{2,1,0:T(8,128)(2,1)} %get-tuple-element.29), channel_id=1, source_target_pairs={{0,1},{4,5},{1,0},{5,4},{2,3},{6,7},{3,2},{7,6},{8,9},{12,13},{9,8... | collective-permute-start | bytes 3145736 | tf_op jit(solution)/shard_map/ppermute | solution.py:261
  12.1 37.5 %all-to-all-start = ((bf16[16,96,128]{2,1,0:T(8,128)(2,1)}), bf16[16,96,128]{2,1,0:T(8,128)(2,1)S(1)}, u32[]{:S(2)}, u32[]{:S(2)}) async-start(bf16[16,96,128]{2,1,0:T(8,128)(2,1)} %along_z.1), calls=%async_computation | async-start | bytes 786432 | tf_op jit(solution)/shard_map/cond/branch_1_fun/all_to_all | solution.py:276
  31.6 28.1 %collective-permute-start = (bf16[8,64,1024]{2,1,0:T(8,128)(2,1)}, bf16[8,64,1024]{2,1,0:T(8,128)(2,1)}, u32[]{:S(2)}, u32[]{:S(2)}) collective-permute-start(bf16[8,64,1024]{2,1,0:T(8,128)(2,1)} %get-tuple-element.13), channel_id=1, source_target_pairs={{0,4},{4,1},{1,5},{5,0},{2,6},{6,3},{3,7},{7,2},{8,12},{12,9},{9,1... | collective-permute-start | bytes 3145736 | tf_op jit(solution)/shard_map/cond/branch_1_fun/ppermute | solution.py:261
  34.2 26.7 %collective-permute-start.1 = (bf16[8,64,1024]{2,1,0:T(8,128)(2,1)}, bf16[8,64,1024]{2,1,0:T(8,128)(2,1)}, u32[]{:S(2)}, u32[]{:S(2)}) collective-permute-start(bf16[8,64,1024]{2,1,0:T(8,128)(2,1)} %get-tuple-element.14), channel_id=1, source_target_pairs={{0,5},{4,0},{1,4},{5,1},{2,7},{6,2},{3,6},{7,3},{8,13},{12,8},{9,1... | collective-permute-start | bytes 3145736 | tf_op jit(solution)/shard_map/cond/branch_1_fun/ppermute | solution.py:261
  50.7 19.3 %copy-start.1 = (bf16[8,64,1024]{2,1,0:T(8,128)(2,1)S(1)}, bf16[8,64,1024]{2,1,0:T(8,128)(2,1)}, u32[]{:S(2)}) copy-start(bf16[8,64,1024]{2,1,0:T(8,128)(2,1)} %get-tuple-element.36) | copy-start | bytes 3145732 | tf_op jit(solution)/shard_map/cond
  50.7 19.3 %all-to-all-start.1 = ((bf16[4,1056,128]{2,1,0:T(8,128)(2,1)}), bf16[4,1056,128]{2,1,0:T(8,128)(2,1)}, u32[]{:S(2)}, u32[]{:S(2)}) async-start(bf16[4,1056,128]{2,1,0:T(8,128)(2,1)} %along_x.1), calls=%async_computation.1 | async-start | bytes 2162688 | tf_op jit(solution)/shard_map/cond/branch_1_fun/all_to_all | solution.py:285
  69.9 4.8 %collective-permute-start.2 = (bf16[4,1056,128]{2,1,0:T(8,128)(2,1)}, bf16[4,1056,128]{2,1,0:T(8,128)(2,1)S(1)}, u32[]{:S(2)}, u32[]{:S(2)}) collective-permute-start(bf16[4,1056,128]{2,1,0:T(8,128)(2,1)} %get-tuple-element.26.s_ref.mine_ref), channel_id=1, source_target_pairs={{0,2},{2,0},{1,3},{3,1},{4,6},{6,4},{5,7},{7,5},{8,10},{10,8},{9,1... | collective-permute-start | bytes 3244040 | tf_op jit(solution)/shard_map/ppermute | solution.py:304
  71.9 2.9 %copy-start = (f32[2,2,32,64]{3,2,1,0:T(8,128)S(1)}, f32[2,2,32,64]{3,2,1,0:T(8,128)}, u32[]{:S(2)}) copy-start(f32[2,2,32,64]{3,2,1,0:T(8,128)} %prev_ref.1) | copy-start | bytes 98308
